TPU v7x, 32 devices: a whole 2x2x4 slice. The times are simulated.
32 devices in a mesh: fsdp: 8 (over z, x), rep: 4 (over y, core).
Axes of the slice: x: 2, y: 2, z: 4, core: 2. Of those that a mesh axis runs over, the one named last changes fastest.
Arguments:
- tokens: bfloat16 [16384, 1024], P(('fsdp', 'rep')), may hold values from -6 to 6
- cond: bfloat16 [64, 768], P(('fsdp', 'rep')), may hold values from -4 to 4
- sigma_idx: int32 [64], P(('fsdp', 'rep')), may hold values from 0 to 63
- pos_rows: int32 [16384], P(('fsdp', 'rep')), may hold values from 0 to 15
- pos_cols: int32 [16384], P(('fsdp', 'rep')), may hold values from 0 to 15
- attn_scale: float32 [16], replicated, may hold values from 6 to 16
- w_mod1: bfloat16 [768, 1024], P('fsdp'), may hold values from -0.21875 to 0.21875
- w_qkv: bfloat16 [1024, 3072], P('fsdp'), may hold values from -0.1875 to 0.1875
- w_out: bfloat16 [1024, 1024], P('fsdp'), may hold values from -0.5 to 0.5
- w_mod2: bfloat16 [768, 1024], P('fsdp'), may hold values from -0.21875 to 0.21875
- w_up: bfloat16 [1024, 6144], P('fsdp'), may hold values from -0.1875 to 0.1875
- w_down: bfloat16 [3072, 1024], P('fsdp'), may hold values from -0.15625 to 0.15625
- cotangent: bfloat16 [16384, 1024], P(('fsdp', 'rep')), may hold values from -6 to 6
Outputs:
- out: bfloat16 [16384, 1024], P(('fsdp', 'rep'))
- d_tokens: bfloat16 [16384, 1024], P(('fsdp', 'rep'))
- d_cond: float32 [64, 768], P(('fsdp', 'rep'))
- d_attn_scale: float32 [16], replicated
- g_mod1: float32 [768, 1024], P('fsdp')
- g_qkv: float32 [1024, 3072], P('fsdp')
- g_out: float32 [1024, 1024], P('fsdp')
- g_mod2: float32 [768, 1024], P('fsdp')
- g_up: float32 [1024, 6144], P('fsdp')
- g_down: float32 [3072, 1024], P('fsdp')
All inputs are finite; a program needn't handle non-finite values.
Results may differ from a plain program's by a relative error of at most 0.02.
Values may be sent and summed in bfloat16 or wider, within the bound.
A program may use at most 256 MiB of HBM per device.

v0:
```python
import math

import jax
import jax.numpy as jnp
from jax import lax
from jax.sharding import PartitionSpec as P

GRID = 16
NB = 64


def sigma_weight(bucket):
    level = bucket.astype(jnp.float32) / (NB - 1)
    sigma = jnp.exp(-2.0 + 3.2 * level)
    return 1.0 / (1.0 + 4.0 * sigma * sigma) + 0.25


def ada_norm(values, modulation):
    factor = lax.rsqrt(jnp.mean(values * values, axis=-1, keepdims=True) + 1e-06)
    return values * factor * (1.0 + modulation)[:, None, :]


def axial_rope(values, rows, cols):
    head_dim = values.shape[-1]
    turned = head_dim // 2
    pairs = turned // 2
    quarter = pairs // 2
    steps = jnp.arange(quarter, dtype=jnp.float32)
    freqs = math.pi * jnp.exp(math.log(10.0) * steps / max(quarter - 1, 1))
    row_pos = (rows.astype(jnp.float32) + 0.5) * (2.0 / GRID) - 1.0
    col_pos = (cols.astype(jnp.float32) + 0.5) * (2.0 / GRID) - 1.0
    angles = jnp.concatenate([row_pos[..., None] * freqs, col_pos[..., None] * freqs], axis=-1)
    cosine = jnp.cos(angles)[:, :, None, :]
    sine = jnp.sin(angles)[:, :, None, :]
    first = values[..., :pairs]
    second = values[..., pairs:turned]
    rest = values[..., turned:]
    return jnp.concatenate(
        [first * cosine - second * sine, first * sine + second * cosine, rest], axis=-1
    )


def cosine_rope(query, keys, scale, rows, cols):
    root = jnp.sqrt(scale)[None, None, :, None]
    query_n = query * lax.rsqrt(jnp.sum(query * query, axis=-1, keepdims=True) + 1e-06) * root
    keys_n = keys * lax.rsqrt(jnp.sum(keys * keys, axis=-1, keepdims=True) + 1e-06) * root
    return (axial_rope(query_n, rows, cols), axial_rope(keys_n, rows, cols))


def geglu_gate(upward):
    hidden = upward.shape[-1] // 2
    return upward[..., :hidden] * jax.nn.gelu(upward[..., hidden:], approximate=False)


def attn_probs(query_low, keys_low, log_total):
    scores = jnp.einsum("ilhd,imhd->ihlm", query_low, keys_low, preferred_element_type=jnp.float32)
    return jnp.exp(scores - log_total[..., None])


def local(
    tokens,
    cond,
    sigma_idx,
    pos_rows,
    pos_cols,
    attn_scale,
    w_mod1,
    w_qkv,
    w_out,
    w_mod2,
    w_up,
    w_down,
    cotangent,
):
    images = cond.shape[0]
    total_rows = tokens.shape[0]
    length = total_rows // images
    width = tokens.shape[1]
    heads = attn_scale.shape[0]
    head_dim = width // heads
    weights = (w_mod1, w_qkv, w_out, w_mod2, w_up, w_down)
    gathered = (
        lax.all_gather(weights[0], "fsdp", axis=0, tiled=True),
        lax.all_gather(weights[1], "fsdp", axis=0, tiled=True),
        lax.all_gather(weights[2], "fsdp", axis=0, tiled=True),
        lax.all_gather(weights[3], "fsdp", axis=0, tiled=True),
        lax.all_gather(weights[4], "fsdp", axis=0, tiled=True),
        lax.all_gather(weights[5], "fsdp", axis=0, tiled=True),
    )
    full_mod1, full_qkv, full_out, full_mod2, full_up, full_down = gathered
    rows = pos_rows.reshape(images, length)
    cols = pos_cols.reshape(images, length)
    inputs = tokens.astype(jnp.float32).reshape(images, length, width)
    mod_one = jnp.dot(cond, full_mod1, preferred_element_type=jnp.float32)
    normed = ada_norm(inputs, mod_one).astype(jnp.bfloat16).reshape(total_rows, width)
    project = jnp.dot(normed, full_qkv, preferred_element_type=jnp.float32).reshape(
        images, length, 3 * width
    )
    query = project[..., :width].reshape(images, length, heads, head_dim)
    keys = project[..., width : 2 * width].reshape(images, length, heads, head_dim)
    value_low = (
        project[..., 2 * width :].reshape(images, length, heads, head_dim).astype(jnp.bfloat16)
    )
    query_rot, keys_rot = cosine_rope(query, keys, attn_scale, rows, cols)
    query_low = query_rot.astype(jnp.bfloat16)
    keys_low = keys_rot.astype(jnp.bfloat16)
    scores = jnp.einsum("ilhd,imhd->ihlm", query_low, keys_low, preferred_element_type=jnp.float32)
    log_total = jax.nn.logsumexp(scores, axis=-1)
    probs_low = jnp.exp(scores - log_total[..., None]).astype(jnp.bfloat16)
    attended = jnp.einsum(
        "ihlm,imhd->ilhd", probs_low, value_low, preferred_element_type=jnp.float32
    )
    attended_low = attended.reshape(total_rows, width).astype(jnp.bfloat16)
    projected = jnp.dot(attended_low, full_out, preferred_element_type=jnp.float32)
    middle = inputs + projected.reshape(images, length, width)
    mod_two = jnp.dot(cond, full_mod2, preferred_element_type=jnp.float32)
    normed_two = ada_norm(middle, mod_two).astype(jnp.bfloat16).reshape(total_rows, width)
    upward = jnp.dot(normed_two, full_up, preferred_element_type=jnp.float32)
    hidden_low = geglu_gate(upward).astype(jnp.bfloat16)
    lowered = jnp.dot(hidden_low, full_down, preferred_element_type=jnp.float32)
    result = (middle.reshape(total_rows, width) + lowered).astype(jnp.bfloat16)
    back_mod1, back_qkv, back_out, back_mod2, back_up, back_down = (
        lax.all_gather(weights[0], "fsdp", axis=0, tiled=True),
        lax.all_gather(weights[1], "fsdp", axis=0, tiled=True),
        lax.all_gather(weights[2], "fsdp", axis=0, tiled=True),
        lax.all_gather(weights[3], "fsdp", axis=0, tiled=True),
        lax.all_gather(weights[4], "fsdp", axis=0, tiled=True),
        lax.all_gather(weights[5], "fsdp", axis=0, tiled=True),
    )
    factor = sigma_weight(sigma_idx)
    grad_out = cotangent.astype(jnp.float32).reshape(images, length, width) * factor[:, None, None]
    down_low = grad_out.reshape(total_rows, width).astype(jnp.bfloat16)
    grad_down = jnp.einsum("tf,td->fd", hidden_low, down_low, preferred_element_type=jnp.float32)
    grad_hidden = jnp.einsum("td,fd->tf", down_low, back_down, preferred_element_type=jnp.float32)
    unused, gate_back = jax.vjp(geglu_gate, upward)
    upward_low = gate_back(grad_hidden)[0].astype(jnp.bfloat16)
    grad_up = jnp.einsum("td,tf->df", normed_two, upward_low, preferred_element_type=jnp.float32)
    grad_normed_two = jnp.einsum(
        "tf,df->td", upward_low, back_up, preferred_element_type=jnp.float32
    )
    unused, norm_back_two = jax.vjp(ada_norm, middle, mod_two)
    grad_mid_norm, grad_mod_two = norm_back_two(grad_normed_two.reshape(images, length, width))
    grad_middle = grad_out + grad_mid_norm
    mod_two_low = grad_mod_two.astype(jnp.bfloat16)
    grad_mod2 = jnp.einsum("ic,id->cd", cond, mod_two_low, preferred_element_type=jnp.float32)
    grad_cond = jnp.einsum("id,cd->ic", mod_two_low, back_mod2, preferred_element_type=jnp.float32)
    proj_low = grad_middle.reshape(total_rows, width).astype(jnp.bfloat16)
    grad_outw = jnp.einsum("td,te->de", attended_low, proj_low, preferred_element_type=jnp.float32)
    grad_att = jnp.einsum("te,de->td", proj_low, back_out, preferred_element_type=jnp.float32)
    att_low = grad_att.astype(jnp.bfloat16).reshape(images, length, heads, head_dim)
    probs = attn_probs(query_low, keys_low, log_total)
    grad_probs = jnp.einsum(
        "ilhd,imhd->ihlm", att_low, value_low, preferred_element_type=jnp.float32
    )
    grad_value = jnp.einsum(
        "ihlm,ilhd->imhd", probs.astype(jnp.bfloat16), att_low, preferred_element_type=jnp.float32
    )
    score_low = (probs * (grad_probs - jnp.sum(grad_probs * probs, axis=-1, keepdims=True))).astype(
        jnp.bfloat16
    )
    grad_qrot = jnp.einsum(
        "ihlm,imhd->ilhd", score_low, keys_low, preferred_element_type=jnp.float32
    )
    grad_krot = jnp.einsum(
        "ihlm,ilhd->imhd", score_low, query_low, preferred_element_type=jnp.float32
    )

    def rotary_part(query_in, keys_in, scale_in):
        return cosine_rope(query_in, keys_in, scale_in, rows, cols)

    unused, rope_back = jax.vjp(rotary_part, query, keys, attn_scale)
    grad_query, grad_keys, grad_scale = rope_back((grad_qrot, grad_krot))
    qkv_low = jnp.concatenate(
        [
            grad_query.reshape(total_rows, width),
            grad_keys.reshape(total_rows, width),
            grad_value.reshape(total_rows, width),
        ],
        axis=1,
    ).astype(jnp.bfloat16)
    grad_qkvw = jnp.einsum("td,te->de", normed, qkv_low, preferred_element_type=jnp.float32)
    grad_normed = jnp.einsum("te,de->td", qkv_low, back_qkv, preferred_element_type=jnp.float32)
    unused, norm_back_one = jax.vjp(ada_norm, inputs, mod_one)
    grad_in_norm, grad_mod_one = norm_back_one(grad_normed.reshape(images, length, width))
    grad_tokens = (grad_middle + grad_in_norm).reshape(total_rows, width).astype(jnp.bfloat16)
    mod_one_low = grad_mod_one.astype(jnp.bfloat16)
    grad_mod1 = jnp.einsum("ic,id->cd", cond, mod_one_low, preferred_element_type=jnp.float32)
    grad_cond = grad_cond + jnp.einsum(
        "id,cd->ic", mod_one_low, back_mod1, preferred_element_type=jnp.float32
    )
    grads = (grad_mod1, grad_qkvw, grad_outw, grad_mod2, grad_up, grad_down)
    shard_sums = (
        lax.psum_scatter(grads[0], "fsdp", scatter_dimension=0, tiled=True),
        lax.psum_scatter(grads[1], "fsdp", scatter_dimension=0, tiled=True),
        lax.psum_scatter(grads[2], "fsdp", scatter_dimension=0, tiled=True),
        lax.psum_scatter(grads[3], "fsdp", scatter_dimension=0, tiled=True),
        lax.psum_scatter(grads[4], "fsdp", scatter_dimension=0, tiled=True),
        lax.psum_scatter(grads[5], "fsdp", scatter_dimension=0, tiled=True),
    )
    summed = (
        lax.psum(shard_sums[0].astype(jnp.bfloat16), "rep").astype(jnp.float32),
        lax.psum(shard_sums[1].astype(jnp.bfloat16), "rep").astype(jnp.float32),
        lax.psum(shard_sums[2].astype(jnp.bfloat16), "rep").astype(jnp.float32),
        lax.psum(shard_sums[3].astype(jnp.bfloat16), "rep").astype(jnp.float32),
        lax.psum(shard_sums[4].astype(jnp.bfloat16), "rep").astype(jnp.float32),
        lax.psum(shard_sums[5].astype(jnp.bfloat16), "rep").astype(jnp.float32),
    )
    scale_total = lax.psum(grad_scale, ("fsdp", "rep"))
    return (
        result,
        grad_tokens,
        grad_cond,
        scale_total,
        summed[0],
        summed[1],
        summed[2],
        summed[3],
        summed[4],
        summed[5],
    )


def solution(mesh):
    placed = (
        P(("fsdp", "rep"), None),
        P(("fsdp", "rep"), None),
        P(("fsdp", "rep")),
        P(("fsdp", "rep")),
        P(("fsdp", "rep")),
        P(),
        P("fsdp", None),
        P("fsdp", None),
        P("fsdp", None),
        P("fsdp", None),
        P("fsdp", None),
        P("fsdp", None),
        P(("fsdp", "rep"), None),
    )
    return jax.shard_map(
        local,
        mesh=mesh,
        in_specs=placed,
        out_specs=(
            P(("fsdp", "rep"), None),
            P(("fsdp", "rep"), None),
            P(("fsdp", "rep"), None),
            P(),
            P("fsdp", None),
            P("fsdp", None),
            P("fsdp", None),
            P("fsdp", None),
            P("fsdp", None),
            P("fsdp", None),
        ),
        check_vma=False,
    )
```

profile of v0, /device:TPU:0, one launch (start us, length us, event | category | flops | bytes accessed | tf_op | source)
XLA Modules:
  0.0 1755.7 jit_solution(11140110549193806433)
XLA Ops:
  13.0 44.2 %all-gather.7.cloned.1.call-done = bf16[768,1024]{1,0:T(8,128)(2,1)} async-done(((bf16[96,1024]{1,0:T(8,128)(2,1)}), bf16[768,1024]{1,0:T(8,128)(2,1)}) %all-gather.7.cloned.1.call-update) | async-done | bytes 1572880 | tf_op jit(solution)/shard_map/all_gather | solution.py:83
  59.2 43.2 %all-gather.13.cloned.1.call-done = bf16[768,1024]{1,0:T(8,128)(2,1)} async-done(((bf16[96,1024]{1,0:T(8,128)(2,1)}), bf16[768,1024]{1,0:T(8,128)(2,1)}) %all-gather.13.cloned.1.call-update) | async-done | bytes 1572880 | tf_op jit(solution)/shard_map/all_gather | solution.py:86
  104.1 98.3 %all-gather.9.cloned.1.call-done = bf16[1024,3072]{1,0:T(8,128)(2,1)} async-done(((bf16[128,3072]{1,0:T(8,128)(2,1)}), bf16[1024,3072]{1,0:T(8,128)(2,1)}) %all-gather.9.cloned.1.call-update) | async-done | bytes 6291472 | tf_op jit(solution)/shard_map/all_gather | solution.py:84
  202.4 5.5 fusion.2
  229.2 22.8 %all-gather.11.cloned.1.call-done = bf16[1024,1024]{1,0:T(8,128)(2,1)} async-done(((bf16[128,1024]{1,0:T(8,128)(2,1)}), bf16[1024,1024]{1,0:T(8,128)(2,1)}) %all-gather.11.cloned.1.call-update) | async-done | bytes 2097168 | tf_op jit(solution)/shard_map/all_gather | solution.py:85
  257.8 171.2 %all-gather.15.cloned.1.call-done = bf16[1024,6144]{1,0:T(8,128)(2,1)} async-done(((bf16[128,6144]{1,0:T(8,128)(2,1)}), bf16[1024,6144]{1,0:T(8,128)(2,1)}) %all-gather.15.cloned.1.call-update) | async-done | bytes 12582928 | tf_op jit(solution)/shard_map/all_gather | solution.py:87
  428.9 12.7 fusion.56
  441.7 86.6 %all-gather.17.cloned.1.call-done = bf16[3072,1024]{1,0:T(8,128)(2,1)} async-done(((bf16[384,1024]{1,0:T(8,128)(2,1)}), bf16[3072,1024]{1,0:T(8,128)(2,1)}) %all-gather.17.cloned.1.call-update) | async-done | bytes 6291472 | tf_op jit(solution)/shard_map/all_gather | solution.py:88
  528.2 22.9 %multiply_add_fusion = (f32[512,3072]{1,0:T(8,128)}, f32[512,3072]{1,0:T(8,128)S(1)}, f32[512,3072]{1,0:T(8,128)}) fusion(f32[512,6144]{1,0:T(8,128)} %fusion.56, bf16[3072,1024]{1,0:T(8,128)(2,1)} %all-gather.17.cloned.1.call-done, f32[512]{0:T(512)S(1)} %bitcast.154, bf16[512,1024]{1,0:T(8,128)(2,1)} %param.25), kind=kOutput, calls=%fused_computation.10 | convolution fusion | flops 3336044544 | bytes 38799360 | tf_op jit(solution)/shard_map/td,fd->tf/dot_general | solution.py:134
  551.1 6.5 fusion.21
  557.6 14.3 fusion.29
  597.9 5.2 fusion.25
  605.5 5.9 multiply_reduce_fusion
  647.0 8.7 fusion.57
  656.9 8.6 fusion.31
  666.7 16.8 fusion.28
  685.5 46.1 %reduce-scatter.19.cloned.1.call-done = f32[96,1024]{1,0:T(8,128)} async-done(((f32[768,1024]{1,0:T(8,128)}), f32[96,1024]{1,0:T(8,128)}) %reduce-scatter.19.cloned.1.call-update) | async-done | bytes 393232
  733.5 88.9 %reduce-scatter.13.cloned.1.call-done = f32[128,1024]{1,0:T(8,128)} async-done(((f32[1024,1024]{1,0:T(8,128)}), f32[128,1024]{1,0:T(8,128)}) %reduce-scatter.13.cloned.1.call-update) | async-done | bytes 524304 | tf_op jit(solution)/shard_map/reduce_scatter | solution.py:195
  824.1 209.2 %reduce-scatter.11.cloned.1.call-done = f32[128,3072]{1,0:T(8,128)} async-done(((f32[1024,3072]{1,0:T(8,128)}), f32[128,3072]{1,0:T(8,128)}) %reduce-scatter.11.cloned.1.call-update) | async-done | bytes 1572880 | tf_op jit(solution)/shard_map/reduce_scatter | solution.py:194
  1035.7 208.1 %reduce-scatter.17.cloned.1.call-done = f32[384,1024]{1,0:T(8,128)} async-done(((f32[3072,1024]{1,0:T(8,128)}), f32[384,1024]{1,0:T(8,128)}) %reduce-scatter.17.cloned.1.call-update) | async-done | bytes 1572880 | tf_op jit(solution)/shard_map/reduce_scatter | solution.py:198
  1246.2 404.8 %reduce-scatter.15.cloned.1.call-done = f32[128,6144]{1,0:T(8,128)} async-done(((f32[1024,6144]{1,0:T(8,128)}), f32[128,6144]{1,0:T(8,128)}) %reduce-scatter.15.cloned.1.call-update) | async-done | bytes 3145744 | tf_op jit(solution)/shard_map/reduce_scatter | solution.py:197
  1655.0 40.5 %psum.49 = f32[16]{0:T(128)} all-reduce(f32[16]{0:T(128)S(1)} %divide_multiply_fusion), channel_id=1, replica_groups=mesh['fsdp'=8,'rep'=4] {'fsdp','rep'}, use_global_device_ids=true, to_apply=%region_15.0 | all-reduce | flops 16 | bytes 128 | tf_op jit(solution)/shard_map/psum | solution.py:208
  1700.1 7.5 fusion.18
  1707.6 29.8 %all-reduce.11.cloned.1.call-done = (bf16[96,1024]{0,1:T(8,128)(2,1)}, bf16[128,3072]{1,0:T(8,128)(2,1)}, bf16[128,1024]{1,0:T(8,128)(2,1)}, bf16[96,1024]{0,1:T...) async-done(((bf16[96,1024]{0,1:T(8,128)(2,1)}, bf16[128,3072]{1,0:T(8,128)(2,1)}, bf16[128,1024]{1,0:T(8,128)(2,1)}, bf16[96,1024]{0,1:T(8,128)(2,1)}, ...) | async-done | bytes 3801104 | tf_op jit(solution)/shard_map/psum | solution.py:201
  (244 shorter events, 132.2 us)
Async XLA Ops:
  7.2 50.0 %copy-start = (bf16[2,768]{1,0:T(2,128)(2,1)S(1)}, bf16[2,768]{1,0:T(2,128)(2,1)}, u32[]{:S(2)}) copy-start(bf16[2,768]{1,0:T(2,128)(2,1)} %param.14) | copy-start | bytes 9220
  7.2 49.9 %all-gather.7.cloned.1.call-start = ((), (), s32[]{:S(2)}) async-start(), calls=%async_computation.6 | async-start | bytes 1769472 | tf_op jit(solution)/shard_map/all_gather | solution.py:83
  8.0 94.4 %all-gather.13.cloned.1.call-start = ((), (), s32[]{:S(2)}) async-start(), calls=%async_computation.9 | async-start | bytes 1769472 | tf_op jit(solution)/shard_map/all_gather | solution.py:86
  8.7 193.7 %all-gather.9.cloned.1.call-start = ((), (), s32[]{:S(2)}) async-start(), calls=%async_computation.7 | async-start | bytes 7077888 | tf_op jit(solution)/shard_map/all_gather | solution.py:84
  9.5 242.5 %all-gather.11.cloned.1.call-start = ((), (), s32[]{:S(2)}) async-start(), calls=%async_computation.8 | async-start | bytes 2359296 | tf_op jit(solution)/shard_map/all_gather | solution.py:85
  10.0 418.9 %all-gather.15.cloned.1.call-start = ((), (), s32[]{:S(2)}) async-start(), calls=%async_computation.10 | async-start | bytes 14155776 | tf_op jit(solution)/shard_map/all_gather | solution.py:87
  10.6 517.6 %all-gather.17.cloned.1.call-start = ((), (), s32[]{:S(2)}) async-start(), calls=%async_computation.11 | async-start | bytes 7077888 | tf_op jit(solution)/shard_map/all_gather | solution.py:88
  11.2 672.4 %reduce-scatter.21.cloned.1.call-start = ((), (), s32[]{:S(2)}) async-start(), calls=%async_computation.17 | async-start | bytes 3538944
  11.3 209.2 %copy-start.46 = (f32[16]{0:T(128)}, f32[16]{0:T(128)S(1)}, u32[]{:S(2)}) copy-start(f32[16]{0:T(128)S(1)} %sqrt.4) | copy-start | bytes 196
  11.8 516.4 %copy-start.51 = (f32[1,2,2,128]{3,1,2,0:T(2,128)}, f32[1,2,2,128]{3,1,2,0:T(2,128)S(1)}, u32[]{:S(2)}) copy-start(f32[1,2,2,128]{3,1,2,0:T(2,128)S(1)} %copy.85) | copy-start | bytes 6148
  13.0 208.5 %copy-start.34 = (f32[2,256,16]{1,2,0:T(8,128)}, f32[2,256,16]{1,2,0:T(8,128)S(1)}, u32[]{:S(2)}) copy-start(f32[2,256,16]{1,2,0:T(8,128)S(1)} %get-tuple-element.73) | copy-start | bytes 98308
  58.9 149.1 %copy-start.40 = (f32[2,1024]{1,0:T(2,128)}, f32[2,1024]{1,0:T(2,128)S(1)}, u32[]{:S(2)}) copy-start(f32[2,1024]{1,0:T(2,128)S(1)} %convolution_add_fusion.1) | copy-start | bytes 24580
  59.2 148.8 %copy-start.31 = (bf16[512,1024]{1,0:T(8,128)(2,1)}, bf16[512,1024]{1,0:T(8,128)(2,1)S(1)}, u32[]{:S(2)}) copy-start(bf16[512,1024]{1,0:T(8,128)(2,1)S(1)} %fusion.15) | copy-start | bytes 3145732
  528.2 22.9 %slice-start.2 = ((s8[12582912]{0:T(1024)(128)(4,1)}), s8[4194304]{0:T(1024)(128)(4,1)S(1)}, s32[]{:S(2)}) async-start(s8[12582912]{0:T(1024)(128)(4,1)} %bitcast.131), calls=%async_computation.21 | async-start | bytes 8388608
  528.2 22.9 %slice-start.3 = ((s8[12582912]{0:T(1024)(128)(4,1)}), s8[4194304]{0:T(1024)(128)(4,1)S(1)}, s32[]{:S(2)}) async-start(s8[12582912]{0:T(1024)(128)(4,1)} %bitcast.131), calls=%async_computation.22 | async-start | bytes 8388608
  528.2 22.9 %slice-start.4 = ((s8[12582912]{0:T(1024)(128)(4,1)}), s8[4194304]{0:T(1024)(128)(4,1)S(1)}, s32[]{:S(2)}) async-start(s8[12582912]{0:T(1024)(128)(4,1)} %bitcast.131), calls=%async_computation.23 | async-start | bytes 8388608
  582.0 149.7 %reduce-scatter.19.cloned.1.call-start = ((), (), s32[]{:S(2)}) async-start(), calls=%async_computation.16 | async-start | bytes 3538944
  640.0 182.4 %reduce-scatter.13.cloned.1.call-start = ((), (), s32[]{:S(2)}) async-start(), calls=%async_computation.13 | async-start | bytes 4718592 | tf_op jit(solution)/shard_map/reduce_scatter | solution.py:195
  645.8 387.5 %reduce-scatter.11.cloned.1.call-start = ((), (), s32[]{:S(2)}) async-start(), calls=%async_computation.12 | async-start | bytes 14155776 | tf_op jit(solution)/shard_map/reduce_scatter | solution.py:194
  655.7 588.1 %reduce-scatter.17.cloned.1.call-start = ((), (), s32[]{:S(2)}) async-start(), calls=%async_computation.15 | async-start | bytes 14155776 | tf_op jit(solution)/shard_map/reduce_scatter | solution.py:198
  665.5 985.6 %reduce-scatter.15.cloned.1.call-start = ((), (), s32[]{:S(2)}) async-start(), calls=%async_computation.14 | async-start | bytes 28311552 | tf_op jit(solution)/shard_map/reduce_scatter | solution.py:197
  683.6 1053.8 %all-reduce.11.cloned.1.call-start = ((), (), s32[]{:S(2)}) async-start(), calls=%async_computation.18 | async-start | bytes 7864320 | tf_op jit(solution)/shard_map/psum | solution.py:201
  1654.3 45.8 %copy-start.5 = (f32[2,256,1024]{2,1,0:T(8,128)S(1)}, f32[2,256,1024]{2,1,0:T(8,128)}, u32[]{:S(2)}) copy-start(f32[2,256,1024]{2,1,0:T(8,128)} %copy-done.4) | copy-start | bytes 6291460
  1737.4 8.1 copy-start.33
  (52 other events, 133.4 us)
Sparse Core Ops, SparseCore 0:
  10.3 46.8 all-gather.6
  59.4 42.9 all-gather.12
  104.6 97.8 all-gather.8
  204.4 47.4 all-gather.10
  254.0 174.9 all-gather.14
  431.0 97.2 all-gather.16
  582.1 72.5 reduce-scatter.20
  658.3 73.2 reduce-scatter.18
  735.3 87.0 reduce-scatter.12
  826.2 207.1 reduce-scatter.10
  1037.3 206.4 reduce-scatter.16
  1248.1 402.9 reduce-scatter.14
  1655.2 82.0 all-reduce.10
where the time goes:
time: 1770 us; the launch traced here: 1760 us
  waiting for transfers between devices  1460 us (82%)
  matrix products  141 us (8%)
  local copies, waits for them, and re-layouts  54.8 us (3%)
  other arithmetic  47.1 us (3%)
  blocking collectives  40.5 us (2%)
    reduce_scatter x1, waiting for transfers between devices, local(): lax.psum_scatter(grads[4], 'fsdp', scatter_dimension=0, tiled=True)  405 us
    reduce_scatter x1, waiting for transfers between devices, local(): lax.psum_scatter(grads[1], 'fsdp', scatter_dimension=0, tiled=True)  209 us
    reduce_scatter x1, waiting for transfers between devices, local(): lax.psum_scatter(grads[5], 'fsdp', scatter_dimension=0, tiled=True)  208 us
    all_gather x1, waiting for transfers between devices, local(): lax.all_gather(weights[4], 'fsdp', axis=0, tiled=True)  171 us
    all_gather x1, waiting for transfers between devices, local(): lax.all_gather(weights[1], 'fsdp', axis=0, tiled=True)  98.3 us
    reduce_scatter x1, waiting for transfers between devices, local(): lax.psum_scatter(grads[2], 'fsdp', scatter_dimension=0, tiled=True)  88.9 us
    all_gather x1, waiting for transfers between devices, local(): lax.all_gather(weights[5], 'fsdp', axis=0, tiled=True)  86.6 us
    unnamed x15, waiting for transfers between devices  49.9 us
  transfers between devices with their start and end apart: 13, of which 12 were waited for; matrix products, arithmetic and copies ran while one was open for 9% of the time, Pallas kernels for 0%

commit v1 on v0

v1 whole, which is shorter than its diff:
```python
import functools
import math

import jax
import jax.numpy as jnp
from jax import lax
from jax.experimental import pallas as pl
from jax.experimental.pallas import tpu as pltpu
from jax.sharding import PartitionSpec as P

GRID = 16
NB = 64

MESH = pl.DeviceIdType.MESH
CH = 512

def place():
    f, r = lax.axis_index("fsdp"), lax.axis_index("rep")
    return f // 2, f % 2, r // 2, r % 2

def is_c(i):
    return (i * 3) % 11 >= 11 - 3

def remote(src, dst, send, recv, z, x, y, c):
    return pltpu.make_async_remote_copy(src_ref=src, dst_ref=dst, send_sem=send, recv_sem=recv,
        device_id=(z * 2 + x, y * 2 + c), device_id_type=MESH)

def wait_bytes(ref, sem):
    pltpu.make_async_copy(ref, ref, sem).wait()

def enter(Z, z, x, y, c):
    barrier = pltpu.get_barrier_semaphore()
    for d in range(1, Z):
        pl.semaphore_signal(barrier, inc=1, device_id=((z + d) % Z * 2 + x, y * 2 + c), device_id_type=MESH)
    for where in ((z * 2 + 1 - x, y * 2 + c), (z * 2 + x, (1 - y) * 2 + c), (z * 2 + x, y * 2 + 1 - c)):
        pl.semaphore_signal(barrier, inc=1, device_id=where, device_id_type=MESH)
    pl.semaphore_wait(barrier, Z + 2)

def gather_ops(src, buf, sends, recvs, own):
    n, Z = buf.shape[0], buf.shape[1]
    z, x, y, c = place()
    zs, xs, ys, yt, cs, ct, cu, cv = (sends.at[k] for k in range(8))
    zr, xr, yr, yq, cr, cq, cp, co = (recvs.at[k] for k in range(8))
    def cols_of(width, k):
        return pl.ds(pl.multiple_of(k * width, 128), width)
    def both(i, fn):
        inside = (i >= 0) & (i < n)
        @pl.when(inside & jnp.logical_not(is_c(i)))
        def _(): fn(128, 2 * y + c, False)
        @pl.when(inside & is_c(i))
        def _(): fn(256, c, True)
    def stage_z(i):
        def go(width, k, cc):
            cols = cols_of(width, k)
            for d in range(1, Z):
                remote(src.at[i, :, cols], buf.at[i, z, x, :, cols], zs.at[i], zr.at[i], (z + d) % Z, x, y, c).start()
            remote(src.at[i, :, cols], buf.at[i, z, x, :, cols], xs.at[i], xr.at[i], z, 1 - x, y, c).start()
        both(i, go)
    def others(i, cols, send, recv, *to):
        for d in range(1, Z):
            zz = (z + d) % Z
            remote(buf.at[i, zz, x, :, cols], buf.at[i, zz, x, :, cols], send, recv, *to).start()
    def partner(i, cols, send, recv, *to):
        part = buf.at[i, :, 1 - x, :, cols]
        remote(part, part, send, recv, *to).start()
    def stage_x(i):
        def go(width, k, cc):
            cols = cols_of(width, k)
            wait_bytes(buf.at[i, 0:Z - 1, 0, :, cols], zr.at[i])
            others(i, cols, xs.at[i], xr.at[i], z, 1 - x, y, c)
            if not cc:
                others(i, cols, ys.at[i], yr.at[i], z, x, 1 - y, c)
            others(i, cols, cs.at[i], cr.at[i], z, x, y, 1 - c)
        both(i, go)
    def stage_y(i):
        def go(width, k, cc):
            cols = cols_of(width, k)
            wait_bytes(buf.at[i, :, 0, :, cols], xr.at[i])
            if not cc:
                partner(i, cols, yt.at[i], yq.at[i], z, x, 1 - y, c)
            partner(i, cols, ct.at[i], cq.at[i], z, x, y, 1 - c)
        both(i, go)
    def stage_c(i):
        def go(width, k, cc):
            if cc: return
            cols = cols_of(width, k)
            wait_bytes(buf.at[i, 0:Z - 1, 0, :, cols], yr.at[i])
            wait_bytes(buf.at[i, :, 0, :, cols], yq.at[i])
            mine = cols_of(128, 2 * (1 - y) + c)
            others(i, mine, cu.at[i], cp.at[i], z, x, y, 1 - c)
            partner(i, mine, cv.at[i], co.at[i], z, x, y, 1 - c)
        both(i, go)
    def core_waits(i, one, two, three, four):
        def go(width, k, cc):
            cols = pl.ds(0, width)
            wait_bytes(buf.at[i, 0:Z - 1, 0, :, cols], one.at[i])
            wait_bytes(buf.at[i, :, 0, :, cols], two.at[i])
            if not cc:
                wait_bytes(buf.at[i, 0:Z - 1, 0, :, cols], three.at[i])
                wait_bytes(buf.at[i, :, 0, :, cols], four.at[i])
        both(i, go)
    def ready(i):
        core_waits(i, cr, cq, cp, co)
    def finish():
        def body(i, _):
            def go(width, k, cc):
                cols = cols_of(width, k)
                wait_bytes(buf.at[i, 0:Z - 1, 0, :, cols], zs.at[i])
                wait_bytes(buf.at[i, :, 0, :, cols], xs.at[i])
                if not cc:
                    wait_bytes(buf.at[i, 0:Z - 1, 0, :, cols], ys.at[i])
                    wait_bytes(buf.at[i, :, 0, :, cols], yt.at[i])
            both(i, go)
            core_waits(i, cs, ct, cu, cv)
            return 0
        lax.fori_loop(0, n, body, 0)
    return stage_z, stage_x, stage_y, stage_c, ready, finish

LAG = (0, 2, 4, 6, 7)
def gather_kernel(lag, src, buf, sends, recvs, own):
    n, Z = buf.shape[0], buf.shape[1]
    z, x, y, c = place()
    enter(Z, z, x, y, c)
    keep = pltpu.make_async_copy(src, buf.at[:, z, x], own)
    keep.start()
    stage_z, stage_x, stage_y, stage_c, ready, finish = gather_ops(src, buf, sends, recvs, own)
    def body(t, _):
        stage_z(t - lag[0])
        stage_x(t - lag[1])
        stage_y(t - lag[2])
        stage_c(t - lag[3])
        ready(t - lag[4])
        return 0
    lax.fori_loop(0, n + lag[4], body, 0)
    keep.wait()
    finish()

def gather(src, F, lag=LAG, cid=0):
    n, R, w = src.shape
    return pl.pallas_call(functools.partial(gather_kernel, lag),
        out_shape=jax.ShapeDtypeStruct((n, F // 2, 2, R, w), src.dtype),
        in_specs=[pl.BlockSpec(memory_space=pltpu.HBM)], out_specs=pl.BlockSpec(memory_space=pltpu.HBM),
        scratch_shapes=[pltpu.SemaphoreType.DMA((8, n)), pltpu.SemaphoreType.DMA((8, n)), pltpu.SemaphoreType.DMA],
        compiler_params=pltpu.CompilerParams(collective_id=cid, has_side_effects=True))(src)

SLOTS = 4
def r_is_c(i):
    return (i * 5) % 11 >= 11 - 5

def lanes(k, width):
    return pl.ds(pl.multiple_of(k * width, 128), width)

def plus(a, b):
    return (a.astype(jnp.float32) + b.astype(jnp.float32)).astype(jnp.bfloat16)

def scatter_ops(n, g, rc, ry, rx, rz, rl, out, sends, recvs):
    Z = rc.shape[1]
    z, x, y, c = place()
    def both(i, fn_a, fn_c):
        inside = (i >= 0) & (i < n)
        @pl.when(inside & jnp.logical_not(r_is_c(i)))
        def _(): fn_a()
        @pl.when(inside & r_is_c(i))
        def _(): fn_c()
    def each(fn):
        lax.fori_loop(0, Z, lambda k, _: (fn(k), 0)[1], 0)
    def s0(i):
        @pl.when((i >= 0) & (i < n))
        def _():
            remote(g.at[i % SLOTS, :, :, :, lanes(1 - c, 256)], rc.at[i], sends.at[0, i], recvs.at[0, i], z, x, y, 1 - c).start()
    def free(i):
        @pl.when((i >= 0) & (i < n))
        def _(): wait_bytes(rc.at[i], sends.at[0, i])
    def s1(i):
        def add():
            wait_bytes(rc.at[i], recvs.at[0, i])
            def one(k):
                rc[i, k] = plus(rc[i, k], g[i % SLOTS, k, :, :, lanes(c, 256)])
            each(one)
        def a():
            add()
            remote(rc.at[i, :, :, :, lanes(1 - y, 128)], ry.at[i], sends.at[1, i], recvs.at[1, i], z, x, 1 - y, c).start()
        def cc():
            add()
            remote(rc.at[i, :, 1 - x], rx.at[i], sends.at[2, i], recvs.at[2, i], z, 1 - x, y, c).start()
        both(i, a, cc)
    def s2(i):
        def a():
            wait_bytes(ry.at[i], recvs.at[1, i])
            def one(k):
                ry[i, k] = plus(ry[i, k], rc[i, k, :, :, lanes(y, 128)])
            each(one)
            remote(ry.at[i, :, 1 - x], rx.at[i, :, :, pl.ds(0, 128)], sends.at[2, i], recvs.at[2, i], z, 1 - x, y, c).start()
        both(i, a, lambda: None)
    def s3(i):
        def a():
            wait_bytes(rx.at[i, :, :, pl.ds(0, 128)], recvs.at[2, i])
            def one(k):
                rx[i, k, :, 0:128] = plus(rx[i, k, :, 0:128], ry[i, k, x])
            each(one)
            for d in range(1, Z):
                zz = (z + d) % Z
                remote(rx.at[i, zz, :, pl.ds(0, 128)], rz.at[i, d - 1, :, pl.ds(0, 128)], sends.at[3, i], recvs.at[3, i], zz, x, y, c).start()
        def cc():
            wait_bytes(rx.at[i], recvs.at[2, i])
            def one(k):
                rx[i, k] = plus(rx[i, k], rc[i, k, x])
            each(one)
            for d in range(1, Z):
                zz = (z + d) % Z
                remote(rx.at[i, zz], rz.at[i, d - 1], sends.at[3, i], recvs.at[3, i], zz, x, y, c).start()
        both(i, a, cc)
    def s4(i):
        def total(part):
            s = rx[i, z, :, part].astype(jnp.float32)
            for d in range(1, Z):
                s = s + rz[i, d - 1, :, part].astype(jnp.float32)
            return s.astype(jnp.bfloat16)
        def a():
            wait_bytes(rz.at[i, :, :, pl.ds(0, 128)], recvs.at[3, i])
            mine = lanes(2 * c + y, 128)
            out[i, :, mine] = total(pl.ds(0, 128))
            remote(out.at[i, :, mine], out.at[i, :, mine], sends.at[4, i], recvs.at[4, i], z, x, 1 - y, c).start()
        def cc():
            wait_bytes(rz.at[i], recvs.at[3, i])
            out[i, :, lanes(c, 256)] = total(pl.ds(0, 256))
            remote(out.at[i, :, lanes(c, 256)], rl.at[i], sends.at[4, i], recvs.at[4, i], z, x, 1 - y, c).start()
        both(i, a, cc)
    def s5(i):
        mine = lanes(c, 256)
        def fwd():
            remote(out.at[i, :, mine], out.at[i, :, mine], sends.at[5, i], recvs.at[5, i], z, x, y, 1 - c).start()
        def a():
            wait_bytes(out.at[i, :, pl.ds(0, 128)], recvs.at[4, i])
            fwd()
        def cc():
            wait_bytes(rl.at[i], recvs.at[4, i])
            wait_bytes(rl.at[i], sends.at[4, i])
            out[i, :, mine] = plus(out[i, :, mine], rl[i])
            fwd()
        both(i, a, cc)
    def finish():
        def body(i, _):
            def a():
                wait_bytes(ry.at[i], sends.at[1, i])
                wait_bytes(rx.at[i, :, :, pl.ds(0, 128)], sends.at[2, i])
                wait_bytes(rz.at[i, :, :, pl.ds(0, 128)], sends.at[3, i])
                wait_bytes(out.at[i, :, pl.ds(0, 128)], sends.at[4, i])
            def cc():
                wait_bytes(rx.at[i], sends.at[2, i])
                wait_bytes(rz.at[i], sends.at[3, i])
            both(i, a, cc)
            wait_bytes(rl.at[i], sends.at[5, i])
            wait_bytes(rl.at[i], recvs.at[5, i])
            return 0
        lax.fori_loop(0, n, body, 0)
    return s0, free, s1, s2, s3, s4, s5, finish

RLAG = (0, 1, 3, 5, 7, 9)
def scatter_kernel(lag, gsrc, out, g, rc, ry, rx, rz, rl, sends, recvs, gs):
    n, Z = rc.shape[0], rc.shape[1]
    z, x, y, c = place()
    enter(Z, z, x, y, c)
    s0, free, s1, s2, s3, s4, s5, finish = scatter_ops(n, g, rc, ry, rx, rz, rl, out, sends, recvs)
    def load(i):
        @pl.when(i < n)
        def _(): pltpu.make_async_copy(gsrc.at[i], g.at[i % SLOTS], gs.at[i % SLOTS]).start()
    load(0)
    def body(t, _):
        free(t + 1 - SLOTS)
        load(t + 1)
        @pl.when(t < n)
        def _(): pltpu.make_async_copy(gsrc.at[t], g.at[t % SLOTS], gs.at[t % SLOTS]).wait()
        s0(t - lag[0])
        s1(t - lag[1])
        s2(t - lag[2])
        s3(t - lag[3])
        s4(t - lag[4])
        s5(t - lag[5])
        return 0
    lax.fori_loop(0, n + lag[5] + 1, body, 0)
    finish()

def scatter(gsrc, lag=RLAG, cid=1):
    n, Z, _, R, w = gsrc.shape
    B = jnp.bfloat16
    return pl.pallas_call(functools.partial(scatter_kernel, lag),
        out_shape=jax.ShapeDtypeStruct((n, R, w), B),
        in_specs=[pl.BlockSpec(memory_space=pltpu.HBM)], out_specs=pl.BlockSpec(memory_space=pltpu.VMEM),
        scratch_shapes=[pltpu.VMEM((SLOTS, Z, 2, R, w), B), pltpu.VMEM((n, Z, 2, R, w//2), B), pltpu.VMEM((n, Z, 2, R, w//4), B),
            pltpu.VMEM((n, Z, R, w//2), B), pltpu.VMEM((n, Z-1, R, w//2), B), pltpu.VMEM((n, R, w//2), B),
            pltpu.SemaphoreType.DMA((6, n)), pltpu.SemaphoreType.DMA((6, n)), pltpu.SemaphoreType.DMA((SLOTS,))],
        compiler_params=pltpu.CompilerParams(collective_id=cid, has_side_effects=True, vmem_limit_bytes=58*2**20))(gsrc)


EPS = 1e-06
LOW = jnp.bfloat16
FULL = jnp.float32
VMEM_LIMIT = 60 * 2**20
F_LAG = (0, 2, 3, 5, 6)
W_SLOTS = 3


def nn(a, b):
    return jnp.dot(a, b, preferred_element_type=FULL)


def nt(a, b):
    return lax.dot_general(a, b, (((1,), (1,)), ((), ())), preferred_element_type=FULL)


def tn(a, b):
    return lax.dot_general(a, b, (((0,), (0,)), ((), ())), preferred_element_type=FULL)


def at(k, size):
    return pl.ds(pl.multiple_of(k * size, size), size)


def head_sum(v):
    one = lax.broadcasted_iota(jnp.int32, (128, 128), 0) // 64
    two = lax.broadcasted_iota(jnp.int32, (128, 128), 1) // 64
    same = (one == two).astype(LOW)
    high = v.astype(LOW)
    rest = v - high.astype(FULL)
    return nn(high, same) + nn(rest.astype(LOW), same)


def head_mask(rows, second):
    lane = lax.broadcasted_iota(jnp.int32, (rows, 128), 1)
    return (lane >= 64) if second else (lane < 64)


def turn(v, cosine, sine_up, sine_down):
    return v * cosine + pltpu.roll(v, 16, 1) * sine_up + pltpu.roll(v, 112, 1) * sine_down


def norm_rows(src_ref, mods_ref, side, images, dst_ref, x_ref=None):
    rows, width = src_ref.shape
    length = rows // images
    block = 64
    def body(i, _):
        r = at(i, block)
        v = src_ref[r, :].astype(FULL)
        factor = lax.rsqrt(jnp.mean(v * v, axis=1, keepdims=True) + EPS)
        m = mods_ref[pl.ds(i // (length // block), 1), side * width : (side + 1) * width]
        dst_ref[r, :] = (v * factor * (1.0 + m)).astype(LOW)
        return 0
    lax.fori_loop(0, rows // block, body, 0)


def forward_kernel(
    images, tokens, cparts, wm, cosine, sine_up, sine_down, roots, src,
    buf, out, x1_o, qr_o, kr_o, vb_o, rq_o, rk_o, p_o, o_o, h_o, ga_o, gb_o, mods_o, call_o,
    n1, qkv, rqk, probs, att, x1, n2, hid, ga, gb, up, acc, slots, mods, call, mpart, mrecv,
    sends, recvs, own, wsem, osem, csem, msem, lsem,
):
    n, Z = buf.shape[0], buf.shape[1]
    shards = 2 * Z
    rows, width = tokens.shape
    length = rows // images
    half_heads = width // CH
    z, x, y, c = place()
    f = z * 2 + x
    r = y * 2 + c
    barrier = pltpu.get_barrier_semaphore()
    def greet(d, _):
        pl.semaphore_signal(barrier, inc=1, device_id=((f + d) % shards, r), device_id_type=MESH)
        return 0
    lax.fori_loop(1, shards, greet, 0)
    for where in ((f, (1 - y) * 2 + c), (f, y * 2 + 1 - c)):
        pl.semaphore_signal(barrier, inc=1, device_id=where, device_id_type=MESH)
    pl.semaphore_wait(barrier, shards + 1)
    keep = pltpu.make_async_copy(src, buf.at[:, z, x], own)
    keep.start()
    stage_z, stage_x, stage_y, stage_c, ready, finish = gather_ops(src, buf, sends, recvs, own)

    def give(d, _):
        to = (f + d) % shards
        pltpu.make_async_remote_copy(src_ref=cparts.at[to], dst_ref=call.at[f], send_sem=csem.at[0], recv_sem=csem.at[1],
            device_id=(to, r), device_id_type=MESH).start()
        return 0
    lax.fori_loop(1, shards, give, 0)
    call[f] = cparts[f]

    def load(j):
        return pltpu.make_async_copy(buf.at[j], slots.at[j % W_SLOTS], wsem.at[j % W_SLOTS])

    def step(t):
        stage_z(t - F_LAG[0])
        stage_x(t - F_LAG[1])
        stage_y(t - F_LAG[2])
        stage_c(t - F_LAG[3])
        ready(t - F_LAG[4])
        @pl.when((t >= F_LAG[4]) & (t < n + F_LAG[4]))
        def _(): load(t - F_LAG[4]).start()

    def begin(j):
        step(j + F_LAG[4] + 1)
        load(j).wait()
        return j % W_SLOTS

    def weights(slot):
        return slots[slot].reshape(width, CH)

    step(0)
    step(1)
    wait_bytes(call.at[pl.ds(0, shards - 1)], csem.at[1])
    flat = call[...].reshape(shards * call.shape[1], call.shape[2])
    mpart[...] = nn(flat, wm[...]).reshape(mpart.shape)
    def back(d, _):
        to = (f + d) % shards
        pltpu.make_async_remote_copy(src_ref=mpart.at[to, pl.ds(0, 8)], dst_ref=mrecv.at[f], send_sem=msem.at[0], recv_sem=msem.at[1],
            device_id=(to, r), device_id_type=MESH).start()
        return 0
    lax.fori_loop(1, shards, back, 0)
    mrecv[f] = mpart[f, 0:8]
    step(2)
    step(3)
    wait_bytes(mrecv.at[pl.ds(0, shards - 1)], msem.at[1])
    mods[...] = jnp.sum(mrecv[...], axis=0)
    norm_rows(tokens, mods, 0, images, n1)
    keep.wait()
    lax.fori_loop(4, F_LAG[4] + 1, lambda t, _: (step(t), 0)[1], 0)

    def project(half, _):
        lanes_of = lambda s: pl.ds(pl.multiple_of(half * CH + s * 128, 128), 128)
        for part in range(2):
            slot = begin(half * 3 + part)
            v = nn(n1[...], weights(slot))
            for s in range(CH // 128):
                one = v[:, s * 128 : (s + 1) * 128]
                scale = lax.rsqrt(head_sum(one * one) + EPS) * roots[0:1, lanes_of(s)]
                rqk[part, :, lanes_of(s)] = scale
                qkv[part, :, lanes_of(s)] = turn(one * scale, cosine[...], sine_up[...], sine_down[...]).astype(LOW)
        slot = begin(half * 3 + 2)
        qkv[2, :, at(half, CH)] = nn(n1[...], weights(slot)).astype(LOW)
        def pair(k, _):
            image, s = k // (CH // 128), k % (CH // 128)
            tok = at(image, length)
            lane = pl.ds(pl.multiple_of(half * CH + s * 128, 128), 128)
            q, keys, val = qkv[0, tok, lane], qkv[1, tok, lane], qkv[2, tok, lane]
            total = None
            for second in range(2):
                mask = head_mask(length, second)
                scores = jnp.exp(nt(jnp.where(mask, q, jnp.zeros_like(q)), keys))
                p = (scores * (1.0 / jnp.sum(scores, axis=1, keepdims=True))).astype(LOW)
                probs[half * (CH // 128) + s, image, second] = p
                o = nn(p, jnp.where(mask, val, jnp.zeros_like(val)))
                total = o if total is None else total + o
            att[tok, lane] = total.astype(LOW)
            return 0
        lax.fori_loop(0, images * (CH // 128), pair, 0)
        return 0
    lax.fori_loop(0, half_heads, project, 0)
    outs = [
        (qkv.at[0], qr_o), (qkv.at[1], kr_o), (qkv.at[2], vb_o), (rqk.at[0], rq_o), (rqk.at[1], rk_o), (probs, p_o), (att, o_o),
        (mods, mods_o), (call, call_o),
    ]
    later = [(x1, x1_o), (hid, h_o), (ga, ga_o), (gb, gb_o), (n2, out)]
    copies = [pltpu.make_async_copy(a, b, osem.at[k]) for k, (a, b) in enumerate(outs + later)]
    for k in range(len(outs)):
        copies[k].start()

    at_out = 3 * half_heads
    def project_out(j, _):
        slot = begin(at_out + j)
        lane = at(j, CH)
        x1[:, lane] = tokens[:, lane].astype(FULL) + nn(att[...], weights(slot))
        return 0
    lax.fori_loop(0, half_heads, project_out, 0)
    copies[len(outs)].start()
    norm_rows(x1, mods, 1, images, n2)

    at_up = at_out + half_heads
    def widen(j, _):
        up[...] = nn(n2[...], weights(begin(at_up + 2 * j)))
        gate = nn(n2[...], weights(begin(at_up + 2 * j + 1)))
        lane_of = lambda s: pl.ds(pl.multiple_of(j * CH + s * 128, 128), 128)
        for s in range(CH // 128):
            g = gate[:, s * 128 : (s + 1) * 128]
            u = up[:, s * 128 : (s + 1) * 128]
            phi = 0.5 + 0.5 * lax.erf(g * math.sqrt(0.5))
            gelu = g * phi
            slope = phi + g * (jnp.exp(-0.5 * g * g) * (1.0 / math.sqrt(2.0 * math.pi)))
            hid[:, lane_of(s)] = (u * gelu).astype(LOW)
            ga[:, lane_of(s)] = gelu.astype(LOW)
            gb[:, lane_of(s)] = (u * slope).astype(LOW)
        return 0
    hidden = hid.shape[1]
    lax.fori_loop(0, hidden // CH, widen, 0)
    for k in range(1, 4):
        copies[len(outs) + k].start()

    at_down = at_up + 2 * hidden // CH
    def narrow(k, _):
        for j in range(width // CH):
            slot = begin(at_down + k * (width // CH) + j)
            part = nn(hid[:, at(k, width)], weights(slot))
            cols = slice(j * CH, (j + 1) * CH)
            acc[:, cols] = part + jnp.where(k == 0, x1[:, cols], acc[:, cols])
        return 0
    lax.fori_loop(0, hidden // width, narrow, 0)
    n2[...] = acc[...].astype(LOW)
    copies[-1].start()
    for copy in copies:
        copy.wait()
    finish()
    wait_bytes(call.at[pl.ds(0, shards - 1)], csem.at[0])
    wait_bytes(mrecv.at[pl.ds(0, shards - 1)], msem.at[0])


def forward(tokens, cparts, wm, tables, roots, src, shards, images, hidden):
    rows, width = tokens.shape
    n, R, w = src.shape
    Z = shards // 2
    length = rows // images
    pairs = width // 128
    def array(shape, kind):
        return jax.ShapeDtypeStruct(shape, kind)
    wide = (rows, width)
    out_shape = (
        array((n, Z, 2, R, w), LOW), array(wide, LOW), array(wide, FULL), array(wide, LOW), array(wide, LOW), array(wide, LOW),
        array(wide, FULL), array(wide, FULL), array((pairs, images, 2, length, length), LOW), array(wide, LOW),
        array((rows, hidden), LOW), array((rows, hidden), LOW), array((rows, hidden), LOW), array((8, 2 * width), FULL),
        array(cparts.shape, LOW),
    )
    vm = lambda *shape_kind: pltpu.VMEM(*shape_kind)
    scratch = [
        vm(wide, LOW), vm((3, *wide), LOW), vm((2, *wide), FULL), vm((pairs, images, 2, length, length), LOW), vm(wide, LOW),
        vm(wide, FULL), vm(wide, LOW), vm((rows, hidden), LOW), vm((rows, hidden), LOW), vm((rows, hidden), LOW),
        vm((rows, w), FULL), vm(wide, FULL), vm((W_SLOTS, Z, 2, R, w), LOW), vm((8, 2 * width), FULL), vm(cparts.shape, LOW),
        vm((shards, cparts.shape[1], 2 * width), FULL), vm((shards, 8, 2 * width), FULL),
        pltpu.SemaphoreType.DMA((8, n)), pltpu.SemaphoreType.DMA((8, n)), pltpu.SemaphoreType.DMA,
        pltpu.SemaphoreType.DMA((W_SLOTS,)), pltpu.SemaphoreType.DMA((14,)), pltpu.SemaphoreType.DMA((2,)),
        pltpu.SemaphoreType.DMA((2,)), pltpu.SemaphoreType.DMA,
    ]
    hbm, vmem = pl.BlockSpec(memory_space=pltpu.HBM), pl.BlockSpec(memory_space=pltpu.VMEM)
    return pl.pallas_call(
        functools.partial(forward_kernel, images),
        out_shape=out_shape,
        in_specs=[vmem] * 7 + [hbm],
        out_specs=tuple([hbm] * len(out_shape)),
        scratch_shapes=scratch,
        compiler_params=pltpu.CompilerParams(collective_id=0, has_side_effects=True, vmem_limit_bytes=VMEM_LIMIT),
    )(tokens, cparts, wm, *tables, roots, src)


def prepare(tokens, cond, pos_rows, pos_cols, attn_scale, w_mod1, w_qkv, w_out, w_mod2, w_up, w_down, shards):
    rows, width = w_qkv.shape[0], tokens.shape[1]
    per = width // CH
    blocks = w_down.shape[0] // rows
    qkv = w_qkv.reshape(rows, 3, per, CH).transpose(2, 1, 0, 3).reshape(-1, rows, CH)
    out = w_out.reshape(rows, per, CH).transpose(1, 0, 2)
    up = w_up.reshape(rows, 2, shards, blocks, rows).transpose(0, 1, 3, 2, 4)
    up = up.reshape(rows, 2, -1, CH).transpose(2, 1, 0, 3).reshape(-1, rows, CH)
    down = w_down.reshape(blocks, rows, per, CH).transpose(0, 2, 1, 3).reshape(-1, rows, CH)
    src = jnp.concatenate([qkv, out, up, down])
    images, wide = cond.shape
    own = wide // shards
    cparts = cond.reshape(images, shards, own).transpose(1, 0, 2)
    cparts = jnp.pad(cparts, ((0, 0), (0, 16 - images), (0, 128 - own)))
    wm = jnp.pad(jnp.concatenate([w_mod1, w_mod2], axis=1), ((0, 128 - own), (0, 0)))
    head = width // attn_scale.shape[0]
    roots = jnp.broadcast_to(jnp.repeat(jnp.sqrt(attn_scale), head)[None], (8, width))
    turned = head // 2
    quarter = turned // 4
    steps = jnp.arange(quarter, dtype=FULL)
    freqs = math.pi * jnp.exp(math.log(10.0) * steps / max(quarter - 1, 1))
    row_pos = (pos_rows.astype(FULL) + 0.5) * (2.0 / GRID) - 1.0
    col_pos = (pos_cols.astype(FULL) + 0.5) * (2.0 / GRID) - 1.0
    angles = jnp.concatenate([row_pos[:, None] * freqs, col_pos[:, None] * freqs], axis=1)
    cos, sin = jnp.cos(angles), jnp.sin(angles)
    zero, rest = jnp.zeros_like(sin), jnp.zeros((sin.shape[0], head - turned), FULL)
    def pair(*parts):
        one = jnp.concatenate(parts, axis=1)
        return jnp.concatenate([one, one], axis=1)
    tables = (pair(cos, cos, rest + 1.0), pair(zero, sin, rest), pair(-sin, zero, rest))
    return src, cparts, wm, roots, tables


def split_chunks(w_qkv, w_out, w_up, w_down):
    rows = w_qkv.shape[0]
    def across(w):
        return w.reshape(rows, -1, CH).transpose(1, 0, 2)
    qkv, out, up = across(w_qkv), across(w_out), across(w_up)
    heads = qkv.shape[0] // 3
    qkv = qkv.reshape(3, heads, rows, CH).transpose(1, 0, 2, 3).reshape(-1, rows, CH)
    half = up.shape[0] // 2
    up = up.reshape(2, half, rows, CH).transpose(1, 0, 2, 3).reshape(-1, rows, CH)
    down = w_down.reshape(-1, rows, w_down.shape[1] // CH, CH).transpose(0, 2, 1, 3).reshape(-1, rows, CH)
    return jnp.concatenate([qkv, out, up, down])


def join_chunks(chunks, width, hidden):
    lead = chunks.shape[1:-2]
    rows = chunks.shape[-2]
    per = width // CH
    sizes = [3 * per, per, 2 * hidden // CH]
    qkv, out, up, down = jnp.split(chunks, [sizes[0], sizes[0] + sizes[1], sum(sizes)])
    qkv = jnp.swapaxes(qkv.reshape(per, 3, *qkv.shape[1:]), 0, 1).reshape(qkv.shape)
    up = jnp.swapaxes(up.reshape(-1, 2, *up.shape[1:]), 0, 1).reshape(up.shape)
    def across(w):
        w = jnp.moveaxis(w, 0, -2)
        return w.reshape(math.prod(lead) * rows, -1)
    parts = down.shape[0] // per
    down = down.reshape(parts, per, *down.shape[1:])
    down = jnp.moveaxis(jnp.moveaxis(down, 1, -2), 0, len(lead))
    down = down.reshape(math.prod(lead) * parts * rows, -1)
    return across(qkv), across(out), across(up), down


def cut_grads(g_qkv, g_out, g_up, g_down, shards):
    width, hidden = g_out.shape[1], g_down.shape[0]
    rows = width // shards
    per = width // CH
    def across(g):
        return g.reshape(shards, rows, -1, CH).transpose(2, 0, 1, 3)
    qkv, out, up = across(g_qkv), across(g_out), across(g_up)
    qkv = jnp.swapaxes(qkv.reshape(3, per, *qkv.shape[1:]), 0, 1).reshape(qkv.shape)
    up = jnp.swapaxes(up.reshape(2, -1, *up.shape[1:]), 0, 1).reshape(up.shape)
    down = g_down.reshape(shards, -1, rows, per, CH).transpose(1, 3, 0, 2, 4).reshape(-1, shards, rows, CH)
    chunks = jnp.concatenate([qkv, out, up, down])[::-1]
    return chunks.reshape(-1, shards // 2, 2, rows, CH)


def sigma_weight(bucket):
    level = bucket.astype(jnp.float32) / (NB - 1)
    sigma = jnp.exp(-2.0 + 3.2 * level)
    return 1.0 / (1.0 + 4.0 * sigma * sigma) + 0.25


def ada_norm(values, modulation):
    factor = lax.rsqrt(jnp.mean(values * values, axis=-1, keepdims=True) + 1e-06)
    return values * factor * (1.0 + modulation)[:, None, :]


def axial_rope(values, rows, cols):
    head_dim = values.shape[-1]
    turned = head_dim // 2
    pairs = turned // 2
    quarter = pairs // 2
    steps = jnp.arange(quarter, dtype=jnp.float32)
    freqs = math.pi * jnp.exp(math.log(10.0) * steps / max(quarter - 1, 1))
    row_pos = (rows.astype(jnp.float32) + 0.5) * (2.0 / GRID) - 1.0
    col_pos = (cols.astype(jnp.float32) + 0.5) * (2.0 / GRID) - 1.0
    angles = jnp.concatenate([row_pos[..., None] * freqs, col_pos[..., None] * freqs], axis=-1)
    cosine = jnp.cos(angles)[:, :, None, :]
    sine = jnp.sin(angles)[:, :, None, :]
    first = values[..., :pairs]
    second = values[..., pairs:turned]
    rest = values[..., turned:]
    return jnp.concatenate(
        [first * cosine - second * sine, first * sine + second * cosine, rest], axis=-1
    )


def cosine_rope(query, keys, scale, rows, cols):
    root = jnp.sqrt(scale)[None, None, :, None]
    query_n = query * lax.rsqrt(jnp.sum(query * query, axis=-1, keepdims=True) + 1e-06) * root
    keys_n = keys * lax.rsqrt(jnp.sum(keys * keys, axis=-1, keepdims=True) + 1e-06) * root
    return (axial_rope(query_n, rows, cols), axial_rope(keys_n, rows, cols))


def geglu_gate(upward):
    hidden = upward.shape[-1] // 2
    return upward[..., :hidden] * jax.nn.gelu(upward[..., hidden:], approximate=False)


def attn_probs(query_low, keys_low, log_total):
    scores = jnp.einsum("ilhd,imhd->ihlm", query_low, keys_low, preferred_element_type=jnp.float32)
    return jnp.exp(scores - log_total[..., None])


def local(
    tokens,
    cond,
    sigma_idx,
    pos_rows,
    pos_cols,
    attn_scale,
    w_mod1,
    w_qkv,
    w_out,
    w_mod2,
    w_up,
    w_down,
    cotangent,
):
    images = cond.shape[0]
    total_rows = tokens.shape[0]
    length = total_rows // images
    width = tokens.shape[1]
    heads = attn_scale.shape[0]
    head_dim = width // heads
    shards = lax.axis_size("fsdp")
    width_own, hidden = tokens.shape[1], w_down.shape[0] * shards
    fs = lax.axis_index("fsdp")
    map_rows = w_mod1.shape[0]
    src, cparts, wm, roots, tables = prepare(tokens, cond, pos_rows, pos_cols, attn_scale, w_mod1, w_qkv, w_out, w_mod2, w_up, w_down, shards)
    (chunks, result, x1, qr, kr, vb, rq, rk, probs, att, h_p, ga_p, gb_p, mods, call) = forward(tokens, cparts, wm, tables, roots, src, shards, images, hidden)
    full_qkv, full_out, full_up, full_down = join_chunks(
        chunks.reshape(chunks.shape[0], shards, *chunks.shape[3:]), width_own, hidden
    )
    blocks = hidden // width_own
    def unperm(v):
        return v.reshape(-1, blocks, shards, width_own // shards).transpose(0, 2, 1, 3).reshape(-1, hidden)
    back_qkv, back_out, back_down = full_qkv, full_out, full_down
    back_up = jnp.concatenate([unperm(full_up[:, :hidden]), unperm(full_up[:, hidden:])], axis=1)
    hidden_low, ga, gb = unperm(h_p), unperm(ga_p), unperm(gb_p)
    mod_one, mod_two = mods[:images, :width_own], mods[:images, width_own:]
    inputs = tokens.astype(jnp.float32).reshape(images, length, width)
    normed = ada_norm(inputs, mod_one).astype(jnp.bfloat16).reshape(total_rows, width)
    middle = x1.reshape(images, length, width)
    normed_two = ada_norm(middle, mod_two).astype(jnp.bfloat16).reshape(total_rows, width)
    attended_low = att
    rows = pos_rows.reshape(images, length)
    cols = pos_cols.reshape(images, length)
    project = jnp.dot(normed, full_qkv, preferred_element_type=jnp.float32).reshape(images, length, 3 * width)
    query = project[..., :width].reshape(images, length, heads, head_dim)
    keys = project[..., width : 2 * width].reshape(images, length, heads, head_dim)
    value_low = vb.reshape(images, length, heads, head_dim)
    query_low = qr.reshape(images, length, heads, head_dim)
    keys_low = kr.reshape(images, length, heads, head_dim)
    factor = sigma_weight(sigma_idx)
    grad_out = cotangent.astype(jnp.float32).reshape(images, length, width) * factor[:, None, None]
    down_low = grad_out.reshape(total_rows, width).astype(jnp.bfloat16)
    grad_down = jnp.einsum("tf,td->fd", hidden_low, down_low, preferred_element_type=jnp.float32)
    grad_hidden = jnp.einsum("td,fd->tf", down_low, back_down, preferred_element_type=jnp.float32)
    upward_low = jnp.concatenate([grad_hidden * ga.astype(FULL), grad_hidden * gb.astype(FULL)], axis=1).astype(jnp.bfloat16)
    grad_up = jnp.einsum("td,tf->df", normed_two, upward_low, preferred_element_type=jnp.float32)
    grad_normed_two = jnp.einsum(
        "tf,df->td", upward_low, back_up, preferred_element_type=jnp.float32
    )
    unused, norm_back_two = jax.vjp(ada_norm, middle, mod_two)
    grad_mid_norm, grad_mod_two = norm_back_two(grad_normed_two.reshape(images, length, width))
    grad_middle = grad_out + grad_mid_norm
    mod_two_low = grad_mod_two.astype(jnp.bfloat16)
    proj_low = grad_middle.reshape(total_rows, width).astype(jnp.bfloat16)
    grad_outw = jnp.einsum("td,te->de", attended_low, proj_low, preferred_element_type=jnp.float32)
    grad_att = jnp.einsum("te,de->td", proj_low, back_out, preferred_element_type=jnp.float32)
    att_low = grad_att.astype(jnp.bfloat16).reshape(images, length, heads, head_dim)
    probs = probs.transpose(1, 0, 2, 3, 4).reshape(images, heads, length, length).astype(FULL)
    grad_probs = jnp.einsum(
        "ilhd,imhd->ihlm", att_low, value_low, preferred_element_type=jnp.float32
    )
    grad_value = jnp.einsum(
        "ihlm,ilhd->imhd", probs.astype(jnp.bfloat16), att_low, preferred_element_type=jnp.float32
    )
    score_low = (probs * (grad_probs - jnp.sum(grad_probs * probs, axis=-1, keepdims=True))).astype(
        jnp.bfloat16
    )
    grad_qrot = jnp.einsum(
        "ihlm,imhd->ilhd", score_low, keys_low, preferred_element_type=jnp.float32
    )
    grad_krot = jnp.einsum(
        "ihlm,ilhd->imhd", score_low, query_low, preferred_element_type=jnp.float32
    )

    def rotary_part(query_in, keys_in, scale_in):
        return cosine_rope(query_in, keys_in, scale_in, rows, cols)

    unused, rope_back = jax.vjp(rotary_part, query, keys, attn_scale)
    grad_query, grad_keys, grad_scale = rope_back((grad_qrot, grad_krot))
    qkv_low = jnp.concatenate(
        [
            grad_query.reshape(total_rows, width),
            grad_keys.reshape(total_rows, width),
            grad_value.reshape(total_rows, width),
        ],
        axis=1,
    ).astype(jnp.bfloat16)
    grad_qkvw = jnp.einsum("td,te->de", normed, qkv_low, preferred_element_type=jnp.float32)
    grad_normed = jnp.einsum("te,de->td", qkv_low, back_qkv, preferred_element_type=jnp.float32)
    unused, norm_back_one = jax.vjp(ada_norm, inputs, mod_one)
    grad_in_norm, grad_mod_one = norm_back_one(grad_normed.reshape(images, length, width))
    grad_tokens = (grad_middle + grad_in_norm).reshape(total_rows, width).astype(jnp.bfloat16)
    mod_one_low = grad_mod_one.astype(jnp.bfloat16)
    low = jnp.bfloat16
    grads = cut_grads(grad_qkvw.astype(low), grad_outw.astype(low), grad_up.astype(low), grad_down.astype(low), shards)
    summed = scatter(grads)[::-1].astype(jnp.float32)
    g_qkv, g_out, g_up, g_down = join_chunks(summed, width_own, hidden)
    small = jnp.concatenate([cond, mod_one_low, mod_two_low], axis=1)
    everyone = lax.all_gather(small, ("fsdp", "rep"), axis=0, tiled=True)
    wide = cond.shape[1]
    cond_rows = lax.dynamic_slice_in_dim(everyone[:, :wide], fs * map_rows, map_rows, 1)
    g_mod = lax.dot_general(cond_rows, everyone[:, wide:], (((0,), (0,)), ((), ())), preferred_element_type=jnp.float32)
    g_mod1, g_mod2 = g_mod[:, :width_own], g_mod[:, width_own:]
    rep = lax.axis_index("rep")
    group = everyone[:, wide:].reshape(shards, -1, images, 2 * width_own)
    group = lax.dynamic_index_in_dim(group, rep, 1, keepdims=False)
    d_part = jnp.einsum("fid,cd->fic", group, jnp.concatenate([w_mod1, w_mod2], axis=1), preferred_element_type=jnp.float32)
    grad_cond = lax.all_to_all(d_part, "fsdp", 0, 0, tiled=False)
    grad_cond = jnp.swapaxes(grad_cond, 0, 1).reshape(images, wide)
    scale_total = lax.psum(grad_scale, ("fsdp", "rep"))
    return (
        result,
        grad_tokens,
        grad_cond,
        scale_total,
        g_mod1,
        g_qkv,
        g_out,
        g_mod2,
        g_up,
        g_down,
    )


def solution(mesh):
    placed = (
        P(("fsdp", "rep"), None),
        P(("fsdp", "rep"), None),
        P(("fsdp", "rep")),
        P(("fsdp", "rep")),
        P(("fsdp", "rep")),
        P(),
        P("fsdp", None),
        P("fsdp", None),
        P("fsdp", None),
        P("fsdp", None),
        P("fsdp", None),
        P("fsdp", None),
        P(("fsdp", "rep"), None),
    )
    return jax.shard_map(
        local,
        mesh=mesh,
        in_specs=placed,
        out_specs=(
            P(("fsdp", "rep"), None),
            P(("fsdp", "rep"), None),
            P(("fsdp", "rep"), None),
            P(),
            P("fsdp", None),
            P("fsdp", None),
            P("fsdp", None),
            P("fsdp", None),
            P("fsdp", None),
            P("fsdp", None),
        ),
        check_vma=False,
    )
```

time: 1770 us -> 948 us (0.54)
  waiting for transfers between devices: 1460 us -> 0.01 us
  Pallas kernels: 0 us -> 356 us
  local copies, waits for them, and re-layouts: 54.8 us -> 354 us
  matrix products: 141 us -> 82.3 us
  blocking collectives: 40.5 us -> 83.4 us
    reduce_scatter x4 -> x0, waiting for transfers between devices: 911 us -> none  [the longest x1 405 us: local(): lax.psum_scatter(grads[4], 'fsdp', scatter_dimension=0, tiled=True)]
    all_gather x6 -> x0, waiting for transfers between devices: 466 us -> none  [the longest x1 171 us: local(): lax.all_gather(weights[4], 'fsdp', axis=0, tiled=True)]
    pallas_call x0 -> x2, Pallas kernels: none -> 356 us  [the longest x1 219 us: forward(): pl.pallas_call(functools.partial(forward_kernel, images), out_shape=out_s...]
    reshape x0 -> x24, local copies, waits for them, and re-layouts: none -> 80.2 us  [the longest x1 11.9 us: join_chunks(): down = down.reshape(parts, per, *down.shape[1:])]
    transpose x1 -> x14, local copies, waits for them, and re-layouts: 1.08 us -> 70.7 us  [the longest x6 31.1 us: across(): w = jnp.moveaxis(w, 0, -2)]
    convert_element_type x1 -> x6, local copies, waits for them, and re-layouts: 1.08 us -> 52 us  [the longest x1 16.7 us: local(): grad_up.astype(low)]
    unnamed x15 -> x0, waiting for transfers between devices: 49.9 us -> none
    all_gather x0 -> x1, blocking collectives: none -> 44.8 us  [local(): everyone = lax.all_gather(small, ('fsdp', 'rep'), axis=0, tiled=True)]
  transfers between devices with their start and end apart: 13 -> 1, of which waited for: 12 -> 0; matrix products, arithmetic and copies ran while one was open for 9% -> 20% of each run, Pallas kernels for 0% -> 15%
where the time goes in v1:
time: 948 us; the launch traced here: 936 us
  Pallas kernels  356 us (38%)
  local copies, waits for them, and re-layouts  354 us (37%)
  blocking collectives  83.4 us (9%)
  matrix products  82.3 us (9%)
  other arithmetic  54.2 us (6%)
    pallas_call x1, Pallas kernels, forward(): pl.pallas_call(functools.partial(forward_kernel, images), out_shape=out_s...  219 us
    pallas_call x1, Pallas kernels, scatter(): pl.pallas_call(functools.partial(scatter_kernel, lag), out_shape=jax.Shap...  137 us
    unnamed x125, local copies, waits for them, and re-layouts  61.2 us
    all_gather x1, blocking collectives, local(): everyone = lax.all_gather(small, ('fsdp', 'rep'), axis=0, tiled=True)  44.8 us
    psum x1, blocking collectives, local(): scale_total = lax.psum(grad_scale, ('fsdp', 'rep'))  38.6 us
    split x7, local copies, waits for them, and re-layouts, join_chunks(): jnp.split(chunks, [sizes[0], sizes[0] + sizes[1], sum(sizes)])  32.3 us
    transpose x6, local copies, waits for them, and re-layouts, across(): w = jnp.moveaxis(w, 0, -2)  31.1 us
  transfers between devices with their start and end apart: 1, of which 0 were waited for; matrix products, arithmetic and copies ran while one was open for 20% of the time, Pallas kernels for 15%

profile of v1, /device:TPU:0, one launch (start us, length us, event | category | flops | bytes accessed | tf_op | source)
XLA Modules:
  0.0 935.6 jit_solution(18062233977902900253)
XLA Ops:
  28.4 219.2 %shard_map.204 = (bf16[26,4,2,128,512]{4,3,2,1,0:T(8,128)(2,1)}, bf16[512,1024]{1,0:T(8,128)(2,1)}, f32[512,1024]{1,0:T(8,128)}, bf16[512,1024]{1,0:T(8,128)(2,1...) custom-call(bf16[512,1024]{1,0:T(8,128)(2,1)} %tokens.1, ...), custom_call_target="tpu_custom_call" | custom-call | tf_op jit(solution)/shard_map/pallas_call | solution.py:539
  247.6 10.4 %fusion.69 = (bf16[6,4,2,128,512]{4,3,2,1,0:T(8,128)(2,1)}, bf16[6,4,2,128,512]{4,3,2,1,0:T(8,128)(2,1)}) fusion(bf16[26,4,2,128,512]{4,3,2,1,0:T(8,128)(2,1)} %get-tuple-element.23), kind=kLoop, calls=%fused_computation.137 | loop fusion | bytes 25165824 | tf_op jit(solution)/shard_map/split | solution.py:600
  258.0 10.5 %split.45 = bf16[12,4,2,128,512]{4,3,2,1,0:T(8,128)(2,1)} slice(bf16[26,4,2,128,512]{4,3,2,1,0:T(8,128)(2,1)} %get-tuple-element.23), slice={[8:20], [0:4], [0:2], [0:128], [0:512]} | slice | bytes 25165824 | tf_op jit(solution)/shard_map/split | solution.py:600
  272.1 11.9 %copy.313 = bf16[3,2,8,128,512]{4,1,3,0,2:T(2,128)(2,1)S(1)} copy(bf16[3,2,8,128,512]{4,3,2,1,0:T(8,128)(2,1)} %bitcast.263) | data formatting | bytes 12582912 | tf_op jit(solution)/shard_map/reshape | solution.py:607
  327.1 10.6 %copy.318 = bf16[6,2,8,128,512]{4,3,2,0,1:T(8,128)(2,1)} copy(bf16[6,2,8,128,512]{4,3,2,1,0:T(8,128)(2,1)} %bitcast.241) | data formatting | bytes 25165824 | tf_op jit(solution)/shard_map/reshape | solution.py:602
  337.7 17.3 %copy.319 = bf16[8,128,12,512]{1,0,3,2:T(8,128)(2,1)} copy(bf16[8,128,12,512]{3,1,0,2:T(8,128)(2,1)} %bitcast.243) | data formatting | bytes 25165824 | tf_op jit(solution)/shard_map/transpose | solution.py:604
  372.8 8.5 multiply_convert_fusion.1
  381.3 13.0 %multiply_reduce_fusion.11 = (f32[512]{0:T(512)S(1)}, f32[512]{0:T(512)S(1)}, f32[512,1024]{1,0:T(8,128)}) fusion(f32[512,1024]{1,0:T(8,128)} %get-tuple-element.27, f32[2,1024]{1,0:T(2,128)S(1)} %get-tuple-element.113, bf16[1024,3072]{0,1:T(8,128)(2,1)} %bitcast.284, bf16[1024,3072]{0,1:T(8,128)(2,1)} %bitcast.283, ...), kind=kOutput, calls=%fused_computation.75 | convolution fusion | flops 6482820096 | bytes 23080960 | tf_op jit(solution)/shard_map/tf,df->td/dot_general | solution.py:732
  453.9 9.0 copy.333
  494.6 8.8 multiply_reduce_fusion.3
  508.1 44.8 %all-gather = bf16[32,2,2816]{2,1,0:T(2,128)(2,1)} all-gather(bf16[1,2,2816]{2,1,0:T(2,128)(2,1)S(1)} %maximum_bitcast_fusion), channel_id=1, replica_groups=mesh['fsdp'=8,'rep'=4] {'fsdp','rep'}, dimensions={0}, use_global_device_ids=true | all-gather | bytes 371712 | tf_op jit(solution)/shard_map/all_gather | solution.py:784
  566.9 8.5 convolution_convert_fusion.2
  575.4 8.6 copy.351
  591.1 9.2 copy.353
  600.3 11.3 %convolution_convert_fusion = bf16[1024,6144]{1,0:T(8,128)(2,1)} fusion(bf16[512,1024]{1,0:T(8,128)(2,1)} %get-tuple-element.106, bf16[512,3072]{1,0:T(8,128)(2,1)} %get-tuple-element.101, bf16[512,3072]{1,0:T(8,128)(2,1)S(1)} %copy-done.26), kind=kOutput, calls=%fused_computation.6 | convolution fusion | flops 6461325312 | bytes 19922944 | tf_op jit(solution)/shard_map/td,tf->df/dot_general | solution.py:731
  611.6 16.7 %copy.355 = bf16[1024,6144]{0,1:T(8,128)(2,1)} copy(bf16[1024,6144]{1,0:T(8,128)(2,1)} %convolution_convert_fusion) | data formatting | bytes 25165824 | tf_op jit(solution)/shard_map/convert_element_type | solution.py:780
  628.2 11.9 %copy.396 = bf16[768,8,8,128]{3,2,1,0:T(8,128)(2,1)} copy(bf16[768,8,8,128]{3,1,2,0:T(8,128)(2,1)} %bitcast.245) | data formatting | bytes 25165824
  640.1 16.7 %copy.357 = bf16[6,2,8,128,512]{4,3,2,1,0:T(8,128)(2,1)} copy(bf16[6,2,8,128,512]{3,2,4,0,1:T(8,128)(2,1)} %bitcast.246) | data formatting | bytes 25165824 | tf_op jit(solution)/shard_map/transpose | solution.py:621
  669.5 8.3 convolution_convert_fusion.1
  677.8 11.4 %reshape.460 = bf16[8,3,128,2,512]{4,3,2,1,0:T(2,128)(2,1)} reshape(bf16[3072,1024]{1,0:T(8,128)(2,1)} %convolution_convert_fusion.1) | data formatting | bytes 12582912 | tf_op jit(solution)/shard_map/reshape | solution.py:622
  696.2 18.2 %pad_maximum_fusion = bf16[26,8,128,512]{3,2,1,0:T(8,128)(2,1)} fusion(bf16[6,8,128,512]{3,2,1,0:T(8,128)(2,1)} %bitcast.270, bf16[12,8,128,512]{3,2,1,0:T(8,128)(2,1)} %bitcast.247, bf16[2,8,128,512]{3,2,1,0:T(8,128)(2,1)S(1)} %bitcast.280, bf16[6,8,128,512]{3,2,1,0:T(8,128)(2,1)} %bitcast.269), kind=kLoop, calls=%fused_computation | loop fusion | flops 40894464 | bytes 54525952 | tf_op jit(solution)/shard_map/concatenate | solution.py:623
  714.3 18.6 %rev.6 = bf16[26,8,128,512]{3,2,1,0:T(8,128)(2,1)} reverse(bf16[26,8,128,512]{3,2,1,0:T(8,128)(2,1)} %pad_maximum_fusion), dimensions={0} | reverse | bytes 54525952 | tf_op jit(solution)/shard_map/rev | solution.py:623
  733.0 136.6 %shard_map.205 = bf16[26,128,512]{2,1,0:T(8,128)(2,1)} custom-call(bf16[26,4,2,128,512]{4,3,2,1,0:T(8,128)(2,1)} %bitcast.238), custom_call_target="tpu_custom_call" | custom-call | tf_op jit(solution)/shard_map/pallas_call | solution.py:287
  880.5 38.6 %psum.7 = f32[16]{0:T(128)} all-reduce(f32[16]{0:T(128)S(1)} %divide_multiply_fusion), channel_id=1, replica_groups=mesh['fsdp'=8,'rep'=4] {'fsdp','rep'}, use_global_device_ids=true, to_apply=%region_13.14 | all-reduce | flops 16 | bytes 128 | tf_op jit(solution)/shard_map/psum | solution.py:795
  (252 shorter events, 255.1 us)
Async XLA Ops:
  10.5 7.3 copy-start.38
  14.1 10.7 %copy-start.25 = (bf16[128,3,2,512]{3,0,1,2:T(8,128)(2,1)S(1)}, bf16[128,3,2,512]{3,0,1,2:T(8,128)(2,1)}, u32[]{:S(2)}) copy-start(bf16[128,3,2,512]{3,0,1,2:T(8,128)(2,1)} %copy.306) | copy-start | bytes 2359300
  284.1 4.7 copy-start.24
  320.4 6.6 copy-start.47
  367.5 5.2 slice-start.3
  367.5 5.2 slice-start.4
  367.5 5.4 copy-start.9
  398.6 4.1 copy-start.29
  420.1 8.2 copy-start.31
  430.6 4.2 copy-start.1
  430.6 4.2 copy-start.10
  439.4 5.1 copy-start.11
  444.5 6.2 slice-start.1
  463.2 6.0 copy-start.32
  474.0 4.0 copy-start.5
  474.0 4.0 copy-start.41
  503.4 4.6 copy-start.39
  508.1 54.8 %copy-start.8 = (bf16[2,256,16,64]{1,3,2,0:T(8,128)(2,1)S(1)}, bf16[2,256,16,64]{1,3,2,0:T(8,128)(2,1)}, u32[]{:S(2)}) copy-start(bf16[2,256,16,64]{1,3,2,0:T(8,128)(2,1)} %fusion.26) | copy-start | bytes 3145732
  554.0 11.3 %copy-start.27 = (bf16[64,2816]{1,0:T(8,128)(2,1)}, bf16[64,2816]{1,0:T(8,128)(2,1)S(1)}, u32[]{:S(2)}) copy-start(bf16[64,2816]{1,0:T(8,128)(2,1)S(1)} %reshape.477) | copy-start | bytes 1081348
  559.4 374.1 %all-to-all-start = ((f32[8,2,96]{2,1,0:T(2,128)}), f32[8,2,96]{2,1,0:T(2,128)S(1)}, u32[]{:S(2)}, u32[]{:S(2)}) async-start(f32[8,2,96]{2,1,0:T(2,128)} %copy.346), calls=%async_computation | async-start | bytes 16384 | tf_op jit(solution)/shard_map/all_to_all | solution.py:793
  591.1 9.2 copy-start.26
  640.1 16.7 %copy-start.36 = (bf16[512,1024]{1,0:T(8,128)(2,1)S(1)}, bf16[512,1024]{1,0:T(8,128)(2,1)}, u32[]{:S(2)}) copy-start(bf16[512,1024]{1,0:T(8,128)(2,1)} %copy-done.35) | copy-start | bytes 3145732
  640.1 16.7 %copy-start.46 = (bf16[512,1024]{1,0:T(8,128)(2,1)S(1)}, bf16[512,1024]{1,0:T(8,128)(2,1)}, u32[]{:S(2)}) copy-start(bf16[512,1024]{1,0:T(8,128)(2,1)} %get-tuple-element.32) | copy-start | bytes 3145732
  689.2 7.0 copy-start.16
  (31 other events, 82.5 us)

commit v2 on v1

v2 whole, which is shorter than its diff:
```python
import functools
import math

import jax
import jax.numpy as jnp
from jax import lax
from jax.experimental import pallas as pl
from jax.experimental.pallas import tpu as pltpu
from jax.sharding import PartitionSpec as P

GRID = 16
NB = 64

MESH = pl.DeviceIdType.MESH
CH = 512

def place():
    f, r = lax.axis_index("fsdp"), lax.axis_index("rep")
    return f // 2, f % 2, r // 2, r % 2

def is_c(i):
    return (i * 3) % 11 >= 11 - 3

def remote(src, dst, send, recv, z, x, y, c):
    return pltpu.make_async_remote_copy(src_ref=src, dst_ref=dst, send_sem=send, recv_sem=recv,
        device_id=(z * 2 + x, y * 2 + c), device_id_type=MESH)

def wait_bytes(ref, sem):
    pltpu.make_async_copy(ref, ref, sem).wait()

def gather_ops(src, buf, sends, recvs, own):
    n, Z = buf.shape[0], buf.shape[1]
    z, x, y, c = place()
    zs, xs, ys, yt, cs, ct, cu, cv = (sends.at[k] for k in range(8))
    zr, xr, yr, yq, cr, cq, cp, co = (recvs.at[k] for k in range(8))
    def cols_of(width, k):
        return pl.ds(pl.multiple_of(k * width, 128), width)
    def both(i, fn):
        inside = (i >= 0) & (i < n)
        @pl.when(inside & jnp.logical_not(is_c(i)))
        def _(): fn(128, 2 * y + c, False)
        @pl.when(inside & is_c(i))
        def _(): fn(256, c, True)
    def keep(i):
        return pltpu.make_async_copy(src.at[i], buf.at[i, z, x], own.at[i])
    def stage_z(i):
        @pl.when((i >= 0) & (i < n))
        def _(): keep(i).start()
        def go(width, k, cc):
            cols = cols_of(width, k)
            for d in range(1, Z):
                remote(src.at[i, :, cols], buf.at[i, z, x, :, cols], zs.at[i], zr.at[i], (z + d) % Z, x, y, c).start()
            remote(src.at[i, :, cols], buf.at[i, z, x, :, cols], xs.at[i], xr.at[i], z, 1 - x, y, c).start()
        both(i, go)
    def others(i, cols, send, recv, *to):
        for d in range(1, Z):
            zz = (z + d) % Z
            remote(buf.at[i, zz, x, :, cols], buf.at[i, zz, x, :, cols], send, recv, *to).start()
    def partner(i, cols, send, recv, *to):
        part = buf.at[i, :, 1 - x, :, cols]
        remote(part, part, send, recv, *to).start()
    def stage_x(i):
        def go(width, k, cc):
            cols = cols_of(width, k)
            wait_bytes(buf.at[i, 0:Z - 1, 0, :, cols], zr.at[i])
            others(i, cols, xs.at[i], xr.at[i], z, 1 - x, y, c)
            if not cc:
                others(i, cols, ys.at[i], yr.at[i], z, x, 1 - y, c)
            others(i, cols, cs.at[i], cr.at[i], z, x, y, 1 - c)
        both(i, go)
    def stage_y(i):
        def go(width, k, cc):
            cols = cols_of(width, k)
            wait_bytes(buf.at[i, :, 0, :, cols], xr.at[i])
            if not cc:
                partner(i, cols, yt.at[i], yq.at[i], z, x, 1 - y, c)
            partner(i, cols, ct.at[i], cq.at[i], z, x, y, 1 - c)
        both(i, go)
    def stage_c(i):
        def go(width, k, cc):
            if cc: return
            cols = cols_of(width, k)
            wait_bytes(buf.at[i, 0:Z - 1, 0, :, cols], yr.at[i])
            wait_bytes(buf.at[i, :, 0, :, cols], yq.at[i])
            mine = cols_of(128, 2 * (1 - y) + c)
            others(i, mine, cu.at[i], cp.at[i], z, x, y, 1 - c)
            partner(i, mine, cv.at[i], co.at[i], z, x, y, 1 - c)
        both(i, go)
    def core_waits(i, one, two, three, four):
        def go(width, k, cc):
            cols = pl.ds(0, width)
            wait_bytes(buf.at[i, 0:Z - 1, 0, :, cols], one.at[i])
            wait_bytes(buf.at[i, :, 0, :, cols], two.at[i])
            if not cc:
                wait_bytes(buf.at[i, 0:Z - 1, 0, :, cols], three.at[i])
                wait_bytes(buf.at[i, :, 0, :, cols], four.at[i])
        both(i, go)
    def ready(i):
        @pl.when((i >= 0) & (i < n))
        def _(): keep(i).wait()
        core_waits(i, cr, cq, cp, co)
    def finish():
        def body(i, _):
            def go(width, k, cc):
                cols = cols_of(width, k)
                wait_bytes(buf.at[i, 0:Z - 1, 0, :, cols], zs.at[i])
                wait_bytes(buf.at[i, :, 0, :, cols], xs.at[i])
                if not cc:
                    wait_bytes(buf.at[i, 0:Z - 1, 0, :, cols], ys.at[i])
                    wait_bytes(buf.at[i, :, 0, :, cols], yt.at[i])
            both(i, go)
            core_waits(i, cs, ct, cu, cv)
            return 0
        lax.fori_loop(0, n, body, 0)
    return stage_z, stage_x, stage_y, stage_c, ready, finish


EPS = 1e-06
LOW = jnp.bfloat16
FULL = jnp.float32
VMEM_LIMIT = 60 * 2**20
F_LAG = (0, 2, 3, 5, 6)
W_SLOTS = 3


def nn(a, b):
    return jnp.dot(a, b, preferred_element_type=FULL)


def nt(a, b):
    return lax.dot_general(a, b, (((1,), (1,)), ((), ())), preferred_element_type=FULL)


def tn(a, b):
    return lax.dot_general(a, b, (((0,), (0,)), ((), ())), preferred_element_type=FULL)


def at(k, size):
    return pl.ds(pl.multiple_of(k * size, size), size)


def head_sum(v):
    one = lax.broadcasted_iota(jnp.int32, (128, 128), 0) // 64
    two = lax.broadcasted_iota(jnp.int32, (128, 128), 1) // 64
    same = (one == two).astype(LOW)
    high = v.astype(LOW)
    rest = v - high.astype(FULL)
    return nn(high, same) + nn(rest.astype(LOW), same)


def head_mask(rows, second):
    lane = lax.broadcasted_iota(jnp.int32, (rows, 128), 1)
    return (lane >= 64) if second else (lane < 64)


def turn(v, cosine, sine_up, sine_down):
    return v * cosine + pltpu.roll(v, 16, 1) * sine_up + pltpu.roll(v, 112, 1) * sine_down


def norm_rows(src_ref, mods_ref, side, images, dst_ref, x_ref=None):
    rows, width = src_ref.shape
    length = rows // images
    block = 64
    def body(i, _):
        r = at(i, block)
        v = src_ref[r, :].astype(FULL)
        factor = lax.rsqrt(jnp.mean(v * v, axis=1, keepdims=True) + EPS)
        m = mods_ref[pl.ds(i // (length // block), 1), side * width : (side + 1) * width]
        dst_ref[r, :] = (v * factor * (1.0 + m)).astype(LOW)
        return 0
    lax.fori_loop(0, rows // block, body, 0)


def forward_kernel(
    images, tokens, cparts, wm, cosine, sine_up, sine_down, roots, src,
    buf, out, x1_o, qr_o, kr_o, vb_o, rq_o, rk_o, p_o, o_o, h_o, ga_o, gb_o, mods_o, call_o,
    n1, qkv, rqk, probs, att, x1, n2, hid, ga, gb, up, acc, slots, mods, call, mpart, mrecv,
    sends, recvs, own, wsem, osem, csem, msem, lsem,
):
    n, Z = buf.shape[0], buf.shape[1]
    shards = 2 * Z
    rows, width = tokens.shape
    length = rows // images
    half_heads = width // CH
    z, x, y, c = place()
    f = z * 2 + x
    r = y * 2 + c
    barrier = pltpu.get_barrier_semaphore()
    def greet(d, _):
        pl.semaphore_signal(barrier, inc=1, device_id=((f + d) % shards, r), device_id_type=MESH)
        return 0
    lax.fori_loop(1, shards, greet, 0)
    for where in ((f, (1 - y) * 2 + c), (f, y * 2 + 1 - c)):
        pl.semaphore_signal(barrier, inc=1, device_id=where, device_id_type=MESH)
    pl.semaphore_wait(barrier, shards + 1)
    stage_z, stage_x, stage_y, stage_c, ready, finish = gather_ops(src, buf, sends, recvs, own)

    def give(d, _):
        to = (f + d) % shards
        pltpu.make_async_remote_copy(src_ref=cparts.at[to], dst_ref=call.at[f], send_sem=csem.at[0], recv_sem=csem.at[1],
            device_id=(to, r), device_id_type=MESH).start()
        return 0
    lax.fori_loop(1, shards, give, 0)
    call[f] = cparts[f]

    def load(j):
        return pltpu.make_async_copy(buf.at[j], slots.at[j % W_SLOTS], wsem.at[j % W_SLOTS])

    def step(t):
        stage_z(t - F_LAG[0])
        stage_x(t - F_LAG[1])
        stage_y(t - F_LAG[2])
        stage_c(t - F_LAG[3])
        ready(t - F_LAG[4])
        @pl.when((t >= F_LAG[4]) & (t < n + F_LAG[4]))
        def _(): load(t - F_LAG[4]).start()

    def begin(j):
        step(j + F_LAG[4] + 1)
        load(j).wait()
        return j % W_SLOTS

    def weights(slot):
        return slots[slot].reshape(width, CH)

    step(0)
    step(1)
    wait_bytes(call.at[pl.ds(0, shards - 1)], csem.at[1])
    flat = call[...].reshape(shards * call.shape[1], call.shape[2])
    mpart[...] = nn(flat, wm[...]).reshape(mpart.shape)
    def back(d, _):
        to = (f + d) % shards
        pltpu.make_async_remote_copy(src_ref=mpart.at[to, pl.ds(0, 8)], dst_ref=mrecv.at[f], send_sem=msem.at[0], recv_sem=msem.at[1],
            device_id=(to, r), device_id_type=MESH).start()
        return 0
    lax.fori_loop(1, shards, back, 0)
    mrecv[f] = mpart[f, 0:8]
    step(2)
    step(3)
    wait_bytes(mrecv.at[pl.ds(0, shards - 1)], msem.at[1])
    mods[...] = jnp.sum(mrecv[...], axis=0)
    norm_rows(tokens, mods, 0, images, n1)
    lax.fori_loop(4, F_LAG[4] + 1, lambda t, _: (step(t), 0)[1], 0)

    def project(half, _):
        lanes_of = lambda s: pl.ds(pl.multiple_of(half * CH + s * 128, 128), 128)
        for part in range(2):
            slot = begin(half * 3 + part)
            v = nn(n1[...], weights(slot))
            for s in range(CH // 128):
                one = v[:, s * 128 : (s + 1) * 128]
                scale = lax.rsqrt(head_sum(one * one) + EPS) * roots[0:1, lanes_of(s)]
                rqk[part, :, lanes_of(s)] = scale
                qkv[part, :, lanes_of(s)] = turn(one * scale, cosine[...], sine_up[...], sine_down[...]).astype(LOW)
        slot = begin(half * 3 + 2)
        qkv[2, :, at(half, CH)] = nn(n1[...], weights(slot)).astype(LOW)
        def pair(k, _):
            image, s = k // (CH // 128), k % (CH // 128)
            tok = at(image, length)
            lane = pl.ds(pl.multiple_of(half * CH + s * 128, 128), 128)
            q, keys, val = qkv[0, tok, lane], qkv[1, tok, lane], qkv[2, tok, lane]
            total = None
            for second in range(2):
                mask = head_mask(length, second)
                scores = jnp.exp(nt(jnp.where(mask, q, jnp.zeros_like(q)), keys))
                p = (scores * (1.0 / jnp.sum(scores, axis=1, keepdims=True))).astype(LOW)
                probs[half * (CH // 128) + s, image, second] = p
                o = nn(p, jnp.where(mask, val, jnp.zeros_like(val)))
                total = o if total is None else total + o
            att[tok, lane] = total.astype(LOW)
            return 0
        lax.fori_loop(0, images * (CH // 128), pair, 0)
        return 0
    lax.fori_loop(0, half_heads, project, 0)
    outs = [
        (qkv.at[0], qr_o), (qkv.at[1], kr_o), (qkv.at[2], vb_o), (rqk.at[0], rq_o), (rqk.at[1], rk_o), (probs, p_o), (att, o_o),
        (mods, mods_o), (call, call_o),
    ]
    later = [(x1, x1_o), (hid, h_o), (ga, ga_o), (gb, gb_o), (n2, out)]
    copies = [pltpu.make_async_copy(a, b, osem.at[k]) for k, (a, b) in enumerate(outs + later)]
    for k in range(len(outs)):
        copies[k].start()

    at_out = 3 * half_heads
    def project_out(j, _):
        slot = begin(at_out + j)
        lane = at(j, CH)
        x1[:, lane] = tokens[:, lane].astype(FULL) + nn(att[...], weights(slot))
        return 0
    lax.fori_loop(0, half_heads, project_out, 0)
    copies[len(outs)].start()
    norm_rows(x1, mods, 1, images, n2)

    at_up = at_out + half_heads
    def widen(j, _):
        up[...] = nn(n2[...], weights(begin(at_up + 2 * j)))
        gate = nn(n2[...], weights(begin(at_up + 2 * j + 1)))
        lane_of = lambda s: pl.ds(pl.multiple_of(j * CH + s * 128, 128), 128)
        for s in range(CH // 128):
            g = gate[:, s * 128 : (s + 1) * 128]
            u = up[:, s * 128 : (s + 1) * 128]
            phi = 0.5 + 0.5 * lax.erf(g * math.sqrt(0.5))
            gelu = g * phi
            slope = phi + g * (jnp.exp(-0.5 * g * g) * (1.0 / math.sqrt(2.0 * math.pi)))
            hid[:, lane_of(s)] = (u * gelu).astype(LOW)
            ga[:, lane_of(s)] = gelu.astype(LOW)
            gb[:, lane_of(s)] = (u * slope).astype(LOW)
        return 0
    hidden = hid.shape[1]
    lax.fori_loop(0, hidden // CH, widen, 0)
    for k in range(1, 4):
        copies[len(outs) + k].start()

    at_down = at_up + 2 * hidden // CH
    def narrow(k, _):
        for j in range(width // CH):
            slot = begin(at_down + k * (width // CH) + j)
            part = nn(hid[:, at(k, width)], weights(slot))
            cols = slice(j * CH, (j + 1) * CH)
            acc[:, cols] = part + jnp.where(k == 0, x1[:, cols], acc[:, cols])
        return 0
    lax.fori_loop(0, hidden // width, narrow, 0)
    n2[...] = acc[...].astype(LOW)
    copies[-1].start()
    for copy in copies:
        copy.wait()
    finish()
    wait_bytes(call.at[pl.ds(0, shards - 1)], csem.at[0])
    wait_bytes(mrecv.at[pl.ds(0, shards - 1)], msem.at[0])


def forward(tokens, cparts, wm, tables, roots, src, shards, images, hidden):
    rows, width = tokens.shape
    n, R, w = src.shape
    Z = shards // 2
    length = rows // images
    pairs = width // 128
    def array(shape, kind):
        return jax.ShapeDtypeStruct(shape, kind)
    wide = (rows, width)
    out_shape = (
        array((n, Z, 2, R, w), LOW), array(wide, LOW), array(wide, FULL), array(wide, LOW), array(wide, LOW), array(wide, LOW),
        array(wide, FULL), array(wide, FULL), array((pairs, images, 2, length, length), LOW), array(wide, LOW),
        array((rows, hidden), LOW), array((rows, hidden), LOW), array((rows, hidden), LOW), array((8, 2 * width), FULL),
        array(cparts.shape, LOW),
    )
    vm = lambda *shape_kind: pltpu.VMEM(*shape_kind)
    scratch = [
        vm(wide, LOW), vm((3, *wide), LOW), vm((2, *wide), FULL), vm((pairs, images, 2, length, length), LOW), vm(wide, LOW),
        vm(wide, FULL), vm(wide, LOW), vm((rows, hidden), LOW), vm((rows, hidden), LOW), vm((rows, hidden), LOW),
        vm((rows, w), FULL), vm(wide, FULL), vm((W_SLOTS, Z, 2, R, w), LOW), vm((8, 2 * width), FULL), vm(cparts.shape, LOW),
        vm((shards, cparts.shape[1], 2 * width), FULL), vm((shards, 8, 2 * width), FULL),
        pltpu.SemaphoreType.DMA((8, n)), pltpu.SemaphoreType.DMA((8, n)), pltpu.SemaphoreType.DMA((n,)),
        pltpu.SemaphoreType.DMA((W_SLOTS,)), pltpu.SemaphoreType.DMA((14,)), pltpu.SemaphoreType.DMA((2,)),
        pltpu.SemaphoreType.DMA((2,)), pltpu.SemaphoreType.DMA,
    ]
    hbm, vmem = pl.BlockSpec(memory_space=pltpu.HBM), pl.BlockSpec(memory_space=pltpu.VMEM)
    return pl.pallas_call(
        functools.partial(forward_kernel, images),
        out_shape=out_shape,
        in_specs=[vmem] * 7 + [hbm],
        out_specs=tuple([hbm] * len(out_shape)),
        scratch_shapes=scratch,
        compiler_params=pltpu.CompilerParams(collective_id=0, has_side_effects=True, vmem_limit_bytes=VMEM_LIMIT),
    )(tokens, cparts, wm, *tables, roots, src)


def prepare(tokens, cond, pos_rows, pos_cols, attn_scale, w_mod1, w_qkv, w_out, w_mod2, w_up, w_down, shards):
    rows, width = w_qkv.shape[0], tokens.shape[1]
    per = width // CH
    blocks = w_down.shape[0] // rows
    qkv = w_qkv.reshape(rows, 3, per, CH).transpose(2, 1, 0, 3).reshape(-1, rows, CH)
    out = w_out.reshape(rows, per, CH).transpose(1, 0, 2)
    up = w_up.reshape(rows, 2, shards, blocks, rows).transpose(0, 1, 3, 2, 4)
    up = up.reshape(rows, 2, -1, CH).transpose(2, 1, 0, 3).reshape(-1, rows, CH)
    down = w_down.reshape(blocks, rows, per, CH).transpose(0, 2, 1, 3).reshape(-1, rows, CH)
    src = jnp.concatenate([qkv, out, up, down])
    images, wide = cond.shape
    own = wide // shards
    cparts = cond.reshape(images, shards, own).transpose(1, 0, 2)
    cparts = jnp.pad(cparts, ((0, 0), (0, 8 - images), (0, 128 - own)))
    cparts = jnp.concatenate([cparts, cparts], axis=1)
    wm = jnp.pad(jnp.concatenate([w_mod1, w_mod2], axis=1), ((0, 128 - own), (0, 0)))
    head = width // attn_scale.shape[0]
    roots = jnp.broadcast_to(jnp.repeat(jnp.sqrt(attn_scale), head)[None], (8, width))
    turned = head // 2
    quarter = turned // 4
    steps = jnp.arange(quarter, dtype=FULL)
    freqs = math.pi * jnp.exp(math.log(10.0) * steps / max(quarter - 1, 1))
    row_pos = (pos_rows.astype(FULL) + 0.5) * (2.0 / GRID) - 1.0
    col_pos = (pos_cols.astype(FULL) + 0.5) * (2.0 / GRID) - 1.0
    angles = jnp.concatenate([row_pos[:, None] * freqs, col_pos[:, None] * freqs], axis=1)
    cos, sin = jnp.cos(angles), jnp.sin(angles)
    zero, rest = jnp.zeros_like(sin), jnp.zeros((sin.shape[0], head - turned), FULL)
    def pair(*parts):
        one = jnp.concatenate(parts, axis=1)
        return jnp.concatenate([one, one], axis=1)
    tables = (pair(cos, cos, rest + 1.0), pair(zero, sin, rest), pair(-sin, zero, rest))
    return src, cparts, wm, roots, tables


Q_SLOTS = 9
RING = 7
A_SLOTS = 2
B_SLOTS = 2
B_LAG = (0, 1, 3, 5, 7, 9)


def of_c(i):
    return (i * 5) % 11 >= 6


def rank_c(i):
    return (i * 5) // 11


def rank_a(i):
    return i - rank_c(i)


def plus(a, b):
    return (a.astype(FULL) + b.astype(FULL)).astype(LOW)


def scatter_ops(n, queue, rc, ry, rxa, rxc, rza, rzc, rl, out, sends, recvs, credit):
    Z = rc.shape[1]
    z, x, y, c = place()
    def cols(k, width):
        return pl.ds(pl.multiple_of(k * width, 128), width)
    def both(i, fn_a, fn_c):
        inside = (i >= 0) & (i < n)
        @pl.when(inside & jnp.logical_not(of_c(i)))
        def _(): fn_a(rank_a(i))
        @pl.when(inside & of_c(i))
        def _(): fn_c(rank_c(i))
    def each(fn):
        lax.fori_loop(0, Z, lambda k, _: (fn(k), 0)[1], 0)
    def s0(i):
        @pl.when((i >= 0) & (i < n))
        def _():
            @pl.when(i >= RING)
            def _(): pl.semaphore_wait(credit, 1)
            remote(queue.at[i % Q_SLOTS, :, :, :, cols(1 - c, 256)], rc.at[i % RING], sends.at[0, i], recvs.at[0, i], z, x, y, 1 - c).start()
    def free(i):
        @pl.when(i >= 0)
        def _(): wait_bytes(rc.at[0], sends.at[0, i])
    def s1(i):
        w = i % RING
        def add():
            wait_bytes(rc.at[w], recvs.at[0, i])
            def one(k):
                rc[w, k] = plus(rc[w, k], queue[i % Q_SLOTS, k, :, :, cols(c, 256)])
            each(one)
        def a(k):
            add()
            remote(rc.at[w, :, :, :, cols(1 - y, 128)], ry.at[k], sends.at[1, i], recvs.at[1, i], z, x, 1 - y, c).start()
        def cc(k):
            add()
            remote(rc.at[w, :, 1 - x], rxc.at[k], sends.at[2, i], recvs.at[2, i], z, 1 - x, y, c).start()
        both(i, a, cc)
    def s2(i):
        w = i % RING
        def a(q):
            wait_bytes(ry.at[q], recvs.at[1, i])
            def one(k):
                ry[q, k] = plus(ry[q, k], rc[w, k, :, :, cols(y, 128)])
            each(one)
            remote(ry.at[q, :, 1 - x], rxa.at[q], sends.at[2, i], recvs.at[2, i], z, 1 - x, y, c).start()
        both(i, a, lambda k: None)
    def s3(i):
        w = i % RING
        def across(rx, rz, q):
            for d in range(1, Z):
                zz = (z + d) % Z
                remote(rx.at[q, zz], rz.at[q, d - 1], sends.at[3, i], recvs.at[3, i], zz, x, y, c).start()
        def done():
            @pl.when(i + RING < n)
            def _(): pl.semaphore_signal(credit, inc=1, device_id=(z * 2 + x, y * 2 + 1 - c), device_id_type=MESH)
        def a(q):
            wait_bytes(rxa.at[q], recvs.at[2, i])
            def one(k):
                rxa[q, k] = plus(rxa[q, k], ry[q, k, x])
            each(one)
            across(rxa, rza, q)
            wait_bytes(ry.at[q], sends.at[1, i])
            done()
        def cc(q):
            wait_bytes(rxc.at[q], recvs.at[2, i])
            def one(k):
                rxc[q, k] = plus(rxc[q, k], rc[w, k, x])
            each(one)
            across(rxc, rzc, q)
            wait_bytes(rxc.at[q], sends.at[2, i])
            done()
        both(i, a, cc)
    def total(rx, rz, q):
        s = rx[q, z].astype(FULL)
        for d in range(1, Z):
            s = s + rz[q, d - 1].astype(FULL)
        return s.astype(LOW)
    def s4(i):
        def a(q):
            wait_bytes(rza.at[q], recvs.at[3, i])
            mine = out.at[i, :, cols(2 * c + y, 128)]
            out[i, :, cols(2 * c + y, 128)] = total(rxa, rza, q)
            remote(mine, mine, sends.at[4, i], recvs.at[4, i], z, x, 1 - y, c).start()
        def cc(q):
            wait_bytes(rzc.at[q], recvs.at[3, i])
            mine = out.at[i, :, cols(c, 256)]
            out[i, :, cols(c, 256)] = total(rxc, rzc, q)
            remote(mine, rl.at[q], sends.at[4, i], recvs.at[4, i], z, x, 1 - y, c).start()
        both(i, a, cc)
    def s5(i):
        mine = out.at[i, :, cols(c, 256)]
        def fwd():
            remote(mine, mine, sends.at[5, i], recvs.at[5, i], z, x, y, 1 - c).start()
        def a(q):
            wait_bytes(out.at[i, :, pl.ds(0, 128)], recvs.at[4, i])
            wait_bytes(out.at[i, :, pl.ds(0, 128)], sends.at[4, i])
            fwd()
        def cc(q):
            wait_bytes(rl.at[q], recvs.at[4, i])
            wait_bytes(rl.at[q], sends.at[4, i])
            out[i, :, cols(c, 256)] = plus(out[i, :, cols(c, 256)], rl[q])
            fwd()
        both(i, a, cc)
    def finish():
        def body(i, _):
            def a(q):
                wait_bytes(rxa.at[q], sends.at[2, i])
                wait_bytes(rza.at[q], sends.at[3, i])
            def cc(q):
                wait_bytes(rzc.at[q], sends.at[3, i])
            both(i, a, cc)
            wait_bytes(rl.at[0], sends.at[5, i])
            wait_bytes(rl.at[0], recvs.at[5, i])
            return 0
        lax.fori_loop(0, n, body, 0)
        lax.fori_loop(n - Q_SLOTS, n, lambda i, _: (free(i), 0)[1], 0)
    return s0, free, s1, s2, s3, s4, s5, finish


def backward_kernel(
    images, wimg, cot, tokens, mods, wm, cosine, sine_up, sine_down, roots, call,
    buf, x1_h, qr_h, kr_h, vb_h, rq_h, rk_h, p_h, o_h, h_h, ga_h, gb_h,
    grads, dtok, gmod, dcond, dscale,
    down, hid, ga, gb, x1, nrm, att, acc, dob, slots, aq, ak, av, arq, ark, ap, dmf, dmx, pm, pr, psum, py, dpart, dcr, dsc, dsr,
    queue, rc, ry, rxa, rxc, rza, rzc, rl, sends, recvs, credit, wsem, lsem, asem, msem, osem,
):
    n, Z, R = buf.shape[0], buf.shape[1], buf.shape[3]
    shards = 2 * Z
    rows, width = tokens.shape
    hidden = hid.shape[1]
    length = rows // images
    per = width // CH
    n_down, n_up, n_out = hidden // width * per, 2 * hidden // CH, per
    z, x, y, c = place()
    f = z * 2 + x
    r = y * 2 + c
    barrier = pltpu.get_barrier_semaphore()
    def greet(d, _):
        pl.semaphore_signal(barrier, inc=1, device_id=((f + d) % shards, r), device_id_type=MESH)
        return 0
    lax.fori_loop(1, shards, greet, 0)
    for where in ((f, (1 - y) * 2 + c), (f, y * 2 + 1 - c)):
        pl.semaphore_signal(barrier, inc=1, device_id=where, device_id_type=MESH)
    given = pltpu.make_async_copy(cot, dob, lsem.at[6])
    given.start()
    loads = [pltpu.make_async_copy(a, b, lsem.at[k]) for k, (a, b) in enumerate(
        [(h_h, hid), (ga_h, ga), (gb_h, gb), (x1_h, x1), (o_h, att)])]
    for one in loads:
        one.start()
    def chunk_of(s):
        first = jnp.where(s < n_down, n - n_down + s, 3 * per + n_out + s - n_down)
        last = jnp.where(s < n_down + n_up + n_out, 3 * per + s - n_down - n_up, s - n_down - n_up - n_out)
        return jnp.where(s < n_down + n_up, first, last)
    def load(s):
        return pltpu.make_async_copy(buf.at[chunk_of(s)], slots.at[s % B_SLOTS], wsem.at[s % B_SLOTS])
    load(0).start()
    def weights(s):
        load(s).wait()
        @pl.when(s + 1 < n)
        def _(): load(s + 1).start()
        return slots[s % B_SLOTS].reshape(width, CH)

    s0, free, s1, s2, s3, s4, s5, finish = scatter_ops(n, queue, rc, ry, rxa, rxc, rza, rzc, rl, grads, sends, recvs, credit)
    def step(t):
        s0(t - B_LAG[0])
        s1(t - B_LAG[1])
        s2(t - B_LAG[2])
        s3(t - B_LAG[3])
        s4(t - B_LAG[4])
        s5(t - B_LAG[5])
    def produce(i, left, right):
        free(i - Q_SLOTS)
        queue[i % Q_SLOTS] = tn(left, right).astype(LOW).reshape(Z, 2, R, CH)

    block = 64
    def blocks(fn):
        lax.fori_loop(0, rows // block, lambda i, _: (fn(at(i, block), i // (length // block)), 0)[1], 0)
    def weigh(k, image):
        down[k, :] = (dob[k, :].astype(FULL) * wimg[image]).astype(LOW)
    given.wait()
    blocks(weigh)
    dmf[...] = jnp.zeros_like(dmf)
    dsc[...] = jnp.zeros_like(dsc)
    pl.semaphore_wait(barrier, shards + 1)
    loads[0].wait()

    def narrow(k, _):
        left = hid[:, at(k, width)]
        for j in range(per):
            produce(k * per + j, left, down[:, j * CH : (j + 1) * CH])
        step(k)
        @pl.when(k == 0)
        def _():
            loads[1].wait()
            loads[2].wait()
        for j in range(per):
            part = nt(down[:, j * CH : (j + 1) * CH], weights(k * per + j))
            acc[...] = part if j == 0 else acc[...] + part
        def gate(q, image):
            ga[q, at(k, width)] = (acc[q, :] * ga[q, at(k, width)].astype(FULL)).astype(LOW)
            gb[q, at(k, width)] = (acc[q, :] * gb[q, at(k, width)].astype(FULL)).astype(LOW)
        blocks(gate)
        return 0
    lax.fori_loop(0, n_down // per, narrow, 0)

    loads[3].wait()
    norm_rows(x1, mods, 1, images, nrm)
    acc[...] = jnp.zeros_like(acc)
    done = n_down // per
    def widen(j, _):
        for side, ref in ((0, ga), (1, gb)):
            s = n_down + 2 * j + side
            produce(s, nrm[...], ref[:, at(j, CH)])
            acc[...] += nt(ref[:, at(j, CH)], weights(s))
        t = done + j + jnp.maximum(j - 3, 0)
        step(t)
        @pl.when(j >= 3)
        def _(): step(t + 1)
        return 0
    lax.fori_loop(0, n_up // 2, widen, 0)
    done = done + n_up // 2 + max(n_up // 2 - 3, 0)

    def norm_back(src_ref, side, base, dst):
        def one(q, image):
            v = src_ref[q, :].astype(FULL)
            dn = acc[q, :]
            factor = lax.rsqrt(jnp.mean(v * v, axis=1, keepdims=True) + EPS)
            m = mods[pl.ds(image, 1), side * width : (side + 1) * width]
            g = dn * (1.0 + m)
            mean = jnp.mean(v * g, axis=1, keepdims=True)
            dst(q, base(q, image) + factor * g - v * (factor * factor * factor * mean))
            dmf[pl.ds(side * 8 + image, 1), :] += jnp.sum(v * factor * dn, axis=0, keepdims=True)
        blocks(one)
    def keep_two(q, value):
        x1[q, :] = value
        down[q, :] = value.astype(LOW)
    norm_back(x1, 1, lambda q, image: dob[q, :].astype(FULL) * wimg[image], keep_two)

    step(done)
    done += 1

    loads[4].wait()
    first_out = n_down + n_up
    for j in range(per):
        right = down[:, j * CH : (j + 1) * CH]
        produce(first_out + j, att[...], right)
        part = nt(right, weights(first_out + j))
        acc[...] = part if j == 0 else acc[...] + part
        step(done)
        done += 1
    dob[...] = acc[...].astype(LOW)
    fill = pltpu.make_async_copy(tokens, att, lsem.at[5])
    fill.start()

    pairs_half = CH // 128
    in_half = images * pairs_half
    def spots(k):
        half, rest = k // in_half, k % in_half
        image, s = rest // pairs_half, half * pairs_half + rest % pairs_half
        return image, s, at(image, length), pl.ds(pl.multiple_of(s * 128, 128), 128)
    def fetch(k):
        image, s, tok, lane = spots(k)
        w = k % A_SLOTS
        refs = [(qr_h.at[tok, lane], aq), (kr_h.at[tok, lane], ak), (vb_h.at[tok, lane], av), (rq_h.at[tok, lane], arq), (rk_h.at[tok, lane], ark), (p_h.at[s, image], ap)]
        return [pltpu.make_async_copy(a, b.at[w], asem.at[e, w]) for e, (a, b) in enumerate(refs)]
    for one in fetch(0):
        one.start()
    acc[...] = jnp.zeros_like(acc)
    total_pairs = images * (width // 128)
    first_qkv = first_out + n_out
    def attend(k, _):
        image, s, tok, lane = spots(k)
        w = k % A_SLOTS
        for one in fetch(k):
            one.wait()
        @pl.when(k + 1 < total_pairs)
        def _():
            for one in fetch(k + 1):
                one.start()
        q, keys, val, dout = aq[w], ak[w], av[w], dob[tok, lane]
        zero = jnp.zeros_like(q)
        dq = dk = dv = None
        for second in range(2):
            mask = head_mask(length, second)
            d_one = jnp.where(mask, dout, zero)
            p = ap[w, second]
            pf = p.astype(FULL)
            dp = nt(d_one, val)
            ds = (pf * (dp - jnp.sum(dp * pf, axis=1, keepdims=True))).astype(LOW)
            dv_one = tn(p, d_one)
            dq_one = nn(ds, jnp.where(mask, keys, zero))
            dk_one = tn(ds, jnp.where(mask, q, zero))
            dq, dk, dv = (dq_one, dk_one, dv_one) if dq is None else (dq + dq_one, dk + dk_one, dv + dv_one)
        inverse = 1.0 / (roots[0:1, lane] * roots[0:1, lane])
        hid[tok, pl.ds(pl.multiple_of(2 * width + s * 128, 128), 128)] = dv.astype(LOW)
        gain = None
        for part, (g, v, scale) in enumerate(((dq, q, arq), (dk, keys, ark))):
            v = v.astype(FULL)
            dot = g * v
            gain = dot if gain is None else gain + dot
            g = g - v * (head_sum(dot) * inverse)
            g = g * cosine[tok, :] - pltpu.roll(g, 112, 1) * sine_down[tok, :] - pltpu.roll(g, 16, 1) * sine_up[tok, :]
            hid[tok, pl.ds(pl.multiple_of(part * width + s * 128, 128), 128)] = (g * scale[w]).astype(LOW)
        dsc[0, pl.ds(s, 1), :] += jnp.sum(gain, axis=0, keepdims=True)
        return 0
    def project(half, t):
        def some(k, t):
            attend(half * in_half + 2 * k, 0)
            attend(half * in_half + 2 * k + 1, 0)
            now = ((half == 0) & (k % 2 == 0)) | ((half > 0) & (k % 2 == 1))
            @pl.when(now)
            def _(): step(t)
            return t + now.astype(jnp.int32)
        t = lax.fori_loop(0, in_half // 2, some, t)
        @pl.when(half == 0)
        def _():
            fill.wait()
            norm_rows(att, mods, 0, images, nrm)
        for part in range(3):
            i = first_qkv + half * 3 + part
            cut = hid[:, pl.ds(pl.multiple_of(part * width + half * CH, CH), CH)]
            produce(i, nrm[...], cut)
            acc[...] += nt(cut, weights(i))
            step(t + part)
        return t + 3
    t = lax.fori_loop(0, per, project, jnp.int32(done))

    def keep_one(q, value):
        down[q, :] = value.astype(LOW)
    norm_back(att, 0, lambda q, image: x1[q, :], keep_one)
    result = pltpu.make_async_copy(down, dtok, osem)
    result.start()
    dmx[f] = dmf[...].astype(LOW)
    def share(d, _):
        pltpu.make_async_remote_copy(src_ref=dmx.at[f], dst_ref=dmx.at[f], send_sem=msem.at[0, 0], recv_sem=msem.at[1, 0],
            device_id=((f + d) % shards, r), device_id_type=MESH).start()
        return 0
    lax.fori_loop(1, shards, share, 0)
    def swap(k, *to):
        return remote(dsc.at[k], dsr.at[k], msem.at[0, 2 + k], msem.at[1, 2 + k], *to)
    swap(0, z, 1 - x, y, c).start()
    step(t)
    wait_bytes(dmx.at[pl.ds(0, shards - 1)], msem.at[1, 0])
    flat = dmx[...].reshape(shards * 16, width)
    group = call[...].reshape(shards * 16, 128)
    upper = lax.broadcasted_iota(jnp.int32, group.shape, 0) % 16 < 8
    nothing = jnp.zeros_like(group)
    pm[:, 0:width] = tn(jnp.where(upper, group, nothing), flat).astype(LOW)
    pm[:, width:] = tn(jnp.where(upper, nothing, group), flat).astype(LOW)
    core_swap = remote(pm, pr, msem.at[0, 5], msem.at[1, 5], z, x, y, 1 - c)
    core_swap.start()
    for side in range(2):
        part = nt(flat, wm[:, side * width : (side + 1) * width]).reshape(shards, 16, 128)[:, side * 8 : side * 8 + 8]
        dpart[...] = part if side == 0 else dpart[...] + part
    def back(d, _):
        to = (f + d) % shards
        pltpu.make_async_remote_copy(src_ref=dpart.at[to], dst_ref=dcr.at[f], send_sem=msem.at[0, 6], recv_sem=msem.at[1, 6],
            device_id=(to, r), device_id_type=MESH).start()
        return 0
    lax.fori_loop(1, shards, back, 0)
    dcr[f] = dpart[f]
    def settle(k):
        swap(k, z, x, y, c).wait()
        dsc[k + 1] = dsc[k] + dsr[k]
    settle(0)
    swap(1, z, x, 1 - y, c).start()
    step(t + 1)
    core_swap.wait()
    half_c = pl.ds(pl.multiple_of(c * width, 128), width)
    psum[...] = plus(pm[:, half_c], pr[:, half_c])
    y_swap = remote(psum, py, msem.at[0, 7], msem.at[1, 7], z, x, 1 - y, c)
    y_swap.start()
    settle(1)
    swap(2, z, x, y, 1 - c).start()
    step(t + 2)
    settle(2)
    dsr[3] = dsc[3]
    def round_z(d):
        return remote(dsr.at[3], dsr.at[4 + z], msem.at[0, 8], msem.at[1, 8], (z + d) % Z, x, y, c)
    for d in range(1, Z):
        round_z(d).start()
    dsr[4 + z] = dsc[3]
    step(t + 3)
    y_swap.wait()
    gmod[:, half_c] = plus(psum[...], py[...])
    last = remote(gmod.at[:, half_c], gmod.at[:, half_c], msem.at[0, 9], msem.at[1, 9], z, x, y, 1 - c)
    last.start()
    wait_bytes(dsr.at[pl.ds(4, Z - 1)], msem.at[1, 8])
    total = dsr[4]
    for k in range(1, Z):
        total = total + dsr[4 + k]
    dscale[...] = total
    step(t + 4)
    wait_bytes(dcr.at[pl.ds(0, shards - 1)], msem.at[1, 6])
    dcond[...] = dcr[...]
    lax.fori_loop(t + 5, n + B_LAG[5], lambda s, _: (step(s), 0)[1], 0)
    last.wait()
    wait_bytes(dmx.at[pl.ds(0, shards - 1)], msem.at[0, 0])
    wait_bytes(dcr.at[pl.ds(0, shards - 1)], msem.at[0, 6])
    wait_bytes(dsr.at[pl.ds(4, Z - 1)], msem.at[0, 8])
    result.wait()
    finish()


def backward(wimg, cot, tokens, mods, wm, tables, roots, call, saved):
    images = wimg.shape[0]
    rows, width = tokens.shape
    n, Z, _, R, w = saved[0].shape
    hidden = saved[9].shape[1]
    length = rows // images
    shards = 2 * Z
    n_c = rank_c(n)
    n_a = n - n_c
    vm, dma = pltpu.VMEM, pltpu.SemaphoreType.DMA
    wide = (rows, width)
    slab = (A_SLOTS, length, 128)
    scratch = [
        vm(wide, LOW), vm((rows, hidden), LOW), vm((rows, hidden), LOW), vm((rows, hidden), LOW), vm(wide, FULL), vm(wide, LOW),
        vm(wide, LOW), vm(wide, FULL), vm(wide, LOW), vm((B_SLOTS, Z, 2, R, w), LOW), vm(slab, LOW), vm(slab, LOW), vm(slab, LOW),
        vm(slab, FULL), vm(slab, FULL), vm((A_SLOTS, 2, length, length), LOW), vm((16, width), FULL), vm((shards, 16, width), LOW),
        vm((128, 2 * width), LOW), vm((128, 2 * width), LOW), vm((128, width), LOW), vm((128, width), LOW),
        vm((shards, 8, 128), FULL), vm((shards, 8, 128), FULL), vm((4, width // 128, 128), FULL), vm((4 + Z, width // 128, 128), FULL),
        vm((Q_SLOTS, Z, 2, R, w), LOW), vm((RING, Z, 2, R, w // 2), LOW), vm((n_a, Z, 2, R, w // 4), LOW), vm((n_a, Z, R, w // 4), LOW),
        vm((n_c, Z, R, w // 2), LOW), vm((n_a, Z - 1, R, w // 4), LOW), vm((n_c, Z - 1, R, w // 2), LOW), vm((n_c, R, w // 2), LOW),
        dma((6, n)), dma((6, n)), pltpu.SemaphoreType.REGULAR, dma((B_SLOTS,)), dma((7,)), dma((6, A_SLOTS)), dma((2, 10)), dma,
    ]
    hbm, vmem = pl.BlockSpec(memory_space=pltpu.HBM), pl.BlockSpec(memory_space=pltpu.VMEM)
    smem = pl.BlockSpec(memory_space=pltpu.SMEM)
    array = jax.ShapeDtypeStruct
    return pl.pallas_call(
        functools.partial(backward_kernel, images),
        out_shape=(array((n, R, w), LOW), array(wide, LOW), array((128, 2 * width), LOW), array((shards, 8, 128), FULL), array((width // 128, 128), FULL)),
        in_specs=[smem, hbm, hbm] + [vmem] * 7 + [hbm] * 12,
        out_specs=(vmem, hbm, vmem, vmem, vmem),
        scratch_shapes=scratch,
        compiler_params=pltpu.CompilerParams(collective_id=1, has_side_effects=True, vmem_limit_bytes=VMEM_LIMIT),
    )(wimg, cot, tokens, mods, wm, *tables, roots, call, *saved)


def local(tokens, cond, sigma_idx, pos_rows, pos_cols, attn_scale, w_mod1, w_qkv, w_out, w_mod2, w_up, w_down, cotangent):
    shards = lax.axis_size("fsdp")
    images, wide = cond.shape
    R, width = w_out.shape
    own = w_mod1.shape[0]
    hidden = w_down.shape[0] * shards
    src, cparts, wm, roots, tables = prepare(tokens, cond, pos_rows, pos_cols, attn_scale, w_mod1, w_qkv, w_out, w_mod2, w_up, w_down, shards)
    (chunks, out, x1, qr, kr, vb, rq, rk, probs, att, h, ga, gb, mods, call) = forward(tokens, cparts, wm, tables, roots, src, shards, images, hidden)
    saved = (chunks, x1, qr, kr, vb, rq, rk, probs, att, h, ga, gb)
    grads, d_tokens, g_mod, d_cond, d_scale = backward(sigma_weight(sigma_idx), cotangent, tokens, mods, wm, tables, roots, call, saved)
    d_cond = d_cond[:, :images, :own].transpose(1, 0, 2).reshape(images, wide)
    d_scale = jnp.sum(d_scale.reshape(attn_scale.shape[0], -1), axis=1) / (2.0 * attn_scale)
    per = width // CH
    blocks = w_down.shape[0] // R
    cuts = [blocks * per, blocks * per + 2 * hidden // CH, blocks * per + 2 * hidden // CH + per]
    down, up, proj, qkv = jnp.split(grads.astype(FULL), cuts)
    g_down = down.reshape(blocks, per, R, CH).transpose(0, 2, 1, 3).reshape(blocks * R, width)
    up = up.reshape(-1, 2, R, CH).transpose(2, 1, 0, 3).reshape(R, 2, blocks, shards, R)
    g_up = up.transpose(0, 1, 3, 2, 4).reshape(R, 2 * hidden)
    g_out = proj.transpose(1, 0, 2).reshape(R, width)
    g_qkv = qkv.reshape(per, 3, R, CH).transpose(2, 1, 0, 3).reshape(R, 3 * width)
    g_mod = g_mod[:own].astype(FULL)
    return out, d_tokens, d_cond, d_scale, g_mod[:, :width], g_qkv, g_out, g_mod[:, width:], g_up, g_down


def sigma_weight(bucket):
    level = bucket.astype(jnp.float32) / (NB - 1)
    sigma = jnp.exp(-2.0 + 3.2 * level)
    return 1.0 / (1.0 + 4.0 * sigma * sigma) + 0.25


def solution(mesh):
    placed = (
        P(("fsdp", "rep"), None),
        P(("fsdp", "rep"), None),
        P(("fsdp", "rep")),
        P(("fsdp", "rep")),
        P(("fsdp", "rep")),
        P(),
        P("fsdp", None),
        P("fsdp", None),
        P("fsdp", None),
        P("fsdp", None),
        P("fsdp", None),
        P("fsdp", None),
        P(("fsdp", "rep"), None),
    )
    return jax.shard_map(
        local,
        mesh=mesh,
        in_specs=placed,
        out_specs=(
            P(("fsdp", "rep"), None),
            P(("fsdp", "rep"), None),
            P(("fsdp", "rep"), None),
            P(),
            P("fsdp", None),
            P("fsdp", None),
            P("fsdp", None),
            P("fsdp", None),
            P("fsdp", None),
            P("fsdp", None),
        ),
        check_vma=False,
    )
```

time: 948 us -> 358 us (0.38)
  local copies, waits for them, and re-layouts: 354 us -> 39.1 us
  blocking collectives: 83.4 us -> 0 us
  matrix products: 82.3 us -> 0 us
  Pallas kernels: 356 us -> 304 us
  other arithmetic: 54.2 us -> 9.31 us
    dot_general x15 -> x0, matrix products: 82.3 us -> none  [the longest x1 13 us: local(): jnp.einsum('tf,df->td', upward_low, back_up, preferred_element_type=jnp.f...]
    pallas_call x1, Pallas kernels: 219 us -> 141 us  [forward(): pl.pallas_call(functools.partial(forward_kernel, images), out_shape=out_s...]
    reshape x19 -> x4, local copies, waits for them, and re-layouts: 77.5 us -> 7.2 us  [the longest x1 3.41 us: local(): qkv.reshape(per, 3, R, CH).transpose(2, 1, 0, 3).reshape(R, 3 * width)]
    transpose x12 -> x7, local copies, waits for them, and re-layouts: 69.8 us -> 6.42 us  [the longest x1 2.37 us: local(): qkv.reshape(per, 3, R, CH).transpose(2, 1, 0, 3).reshape(R, 3 * width)]
    convert_element_type x6 -> x0, local copies, waits for them, and re-layouts: 52 us -> none  [the longest x1 16.7 us: local(): grad_up.astype(low)]
    unnamed x125 -> x25, local copies, waits for them, and re-layouts: 61.2 us -> 10.7 us
    all_gather x1 -> x0, blocking collectives: 44.8 us -> none  [local(): everyone = lax.all_gather(small, ('fsdp', 'rep'), axis=0, tiled=True)]
    psum x1 -> x0, blocking collectives: 38.6 us -> none  [local(): scale_total = lax.psum(grad_scale, ('fsdp', 'rep'))]
  transfers between devices with their start and end apart: 1 -> 0, of which waited for: 0 -> 0; matrix products, arithmetic and copies ran while one was open for 20% -> 0% of each run, Pallas kernels for 15% -> 0%
where the time goes in v2:
time: 358 us; the launch traced here: 354 us
  Pallas kernels  304 us (85%)
  local copies, waits for them, and re-layouts  39.1 us (11%)
  other arithmetic  9.31 us (3%)
    pallas_call x1, Pallas kernels, backward(): pl.pallas_call(functools.partial(backward_kernel, images), out_shape=(arr...  163 us
    pallas_call x1, Pallas kernels, forward(): pl.pallas_call(functools.partial(forward_kernel, images), out_shape=out_s...  141 us
    unnamed x25, local copies, waits for them, and re-layouts  10.7 us

profile of v2, /device:TPU:0, one launch (start us, length us, event | category | flops | bytes accessed | tf_op | source)
XLA Modules:
  0.0 353.7 jit_solution(5957225547858613840)
XLA Ops:
  0.7 1.2 fusion.7.wimg
  5.8 1.1 concatenate.31.sine_up
  7.0 1.1 concatenate.32.sine_down
  8.6 1.1 concatenate.30.cosine
  11.1 1.0 copy.69
  12.7 1.0 copy.75
  13.6 2.4 copy.72
  16.9 3.0 pad_maximum_fusion.src
  20.0 140.8 %shard_map.204 = (bf16[26,4,2,128,512]{4,3,2,1,0:T(8,128)(2,1)}, bf16[512,1024]{1,0:T(8,128)(2,1)}, f32[512,1024]{1,0:T(8,128)}, bf16[512,1024]{1,0:T(8,128)(2,1...) custom-call(bf16[512,1024]{1,0:T(8,128)(2,1)} %tokens.3, ...), custom_call_target="tpu_custom_call" | custom-call | tf_op jit(solution)/shard_map/pallas_call | solution.py:358
  160.8 163.3 %shard_map.205 = (bf16[26,128,512]{2,1,0:T(8,128)(2,1)}, bf16[512,1024]{1,0:T(8,128)(2,1)}, bf16[128,2048]{1,0:T(8,128)(2,1)}, f32[8,8,128]{2,1,0:T(8,128)}, f32[8,128]{1,0:T(8,128)}) custom-call(f32[2]{0:T(128)} %fusion.7.wimg, bf16[512,1024]{1,0:T(8,128)(2,1)} %cot.1, bf16[512,1024]{1,0:T(8,128)(2,1)} %tokens.3, f32[8,2048]{1,0:T(8,128)} %get-tuple-element.31.mods, ...), custom_call_target="tpu_custom_call" | custom-call | tf_op jit(solution)/shard_map/pallas_call | solution.py:853
  326.9 1.1 slice_convert_fusion
  328.0 0.9 fusion.9
  328.9 3.5 split.18
  332.4 2.4 copy.79
  334.8 1.8 copy.80
  336.7 3.7 %copy.83 = f32[128,6144]{1,0:T(8,128)} copy(f32[128,6144]{0,1:T(8,128)} %bitcast.40) | data formatting | bytes 6291456
  340.8 1.2 copy.81
  342.0 1.5 copy.84
  343.5 2.4 copy.77
  345.8 3.4 reshape.98
  349.3 1.0 convert_element_type.23
  350.5 1.0 copy.82
  351.5 1.0 copy.89
  352.5 1.0 copy.90
  (52 shorter events, 10.7 us)
Async XLA Ops:
  0.6 7.6 %copy-start.5 = (bf16[128,1024]{1,0:T(8,128)(2,1)S(1)}, bf16[128,1024]{1,0:T(8,128)(2,1)}, u32[]{:S(2)}) copy-start(bf16[128,1024]{1,0:T(8,128)(2,1)} %param.21) | copy-start | bytes 786436
  6.9 2.8 copy-start.6
  6.9 2.8 copy-start.7
  7.0 3.6 %copy-start.3 = (bf16[128,3072]{1,0:T(8,128)(2,1)S(1)}, bf16[128,3072]{1,0:T(8,128)(2,1)}, u32[]{:S(2)}) copy-start(bf16[128,3072]{1,0:T(8,128)(2,1)} %param.20) | copy-start | bytes 2359300
  8.6 3.5 %copy-start.4 = (bf16[384,1024]{1,0:T(8,128)(2,1)S(1)}, bf16[384,1024]{1,0:T(8,128)(2,1)}, u32[]{:S(2)}) copy-start(bf16[384,1024]{1,0:T(8,128)(2,1)} %param.24) | copy-start | bytes 2359300
  160.8 165.6 %copy-start.8 = (f32[16]{0:T(128)S(1)}, f32[16]{0:T(128)}, u32[]{:S(2)}) copy-start(f32[16]{0:T(128)} %param.18) | copy-start | bytes 196
  336.6 3.7 %copy-start = (bf16[26,128,512]{2,1,0:T(8,128)(2,1)S(1)}, bf16[26,128,512]{2,1,0:T(8,128)(2,1)}, u32[]{:S(2)}) copy-start(bf16[26,128,512]{2,1,0:T(8,128)(2,1)} %get-tuple-element.49) | copy-start | bytes 10223620
  350.2 1.3 copy-start.1
  350.2 2.2 copy-start.2
